TPU v7x, 32 devices: a whole 2x2x4 slice. The times are simulated.
32 devices in a mesh: segment: 4 (over y, x), gz: 8 (over z, core).
Axes of the slice: x: 2, y: 2, z: 4, core: 2. Of those that a mesh axis runs over, the one named last changes fastest.
Arguments:
- start_volume: float32 [4, 128, 1024], P(None, 'gz'), may hold values from -6 to 6
- sinogram: float32 [4, 128, 1024], P(None, 'gz'), may hold values from -6 to 6
- offsets: int32 [4, 8], replicated, may hold values from -15 to 15, as said below
- projector: bfloat16 [3, 1024, 1024], replicated, may hold values from -0.109375 to 0.109375
- dual_in: bfloat16 [32, 27], replicated, may hold values from -1.25 to 1.25
- dual_out: bfloat16 [9, 32], replicated, may hold values from -0.375 to 0.375
- primal_in: bfloat16 [64, 54], replicated, may hold values from -0.875 to 0.875
- primal_out: bfloat16 [27, 64], replicated, may hold values from -0.15625 to 0.15625
Outputs:
- volume: float32 [4, 128, 1024], P('segment', 'gz')
Inputs may be any that keep to these rules, and one draw needn't show every extreme that they name: `offsets`: both ends of the range are taken in every draw.
All inputs are finite; a program needn't handle non-finite values.
Results may differ from a plain program's by a relative error of at most 0.005.
Values may be sent and summed in bfloat16 or wider, within the bound.
No kernel may reach another device: no remote copies, remote signals or barrier semaphores. Data moves between devices by JAX's collectives and lax.ppermute only.
A program may use at most 64 MiB of HBM per device.

v0:
```python
import jax
import jax.numpy as jnp
from jax import lax
from jax.sharding import PartitionSpec as P

IMG = 32
NCOL = 128
ITERS = 2


def padded_2(cells, sides, width):
    for axis, dim in sides:
        count = lax.axis_size(axis)
        ends = count - 1
        head = lax.slice_in_dim(cells, 0, width, axis=dim)
        tail = lax.slice_in_dim(cells, cells.shape[dim] - width, cells.shape[dim], axis=dim)
        cells = jnp.concatenate(
            [
                lax.ppermute(tail, axis, [(i, (i + 1) % count) for i in range(ends)]),
                cells,
                lax.ppermute(head, axis, [((i + 1) % count, i) for i in range(ends)]),
            ],
            axis=dim,
        )
    return cells


def as_sent(x):
    return jax.tree.map(lambda a: a.astype(jnp.bfloat16) if a.dtype == jnp.float32 else a, x)


def plane_taps(flavour):
    cell_count = IMG * IMG
    positions = jnp.arange(cell_count, dtype=jnp.int32)
    tap_list = []
    if flavour == 0:
        column_of = positions % NCOL
        for step_size in (-1, 0, 1):
            keep_mask = ((column_of + step_size >= 0) & (column_of + step_size < NCOL)).astype(
                jnp.float32
            )
            tap_list.append((step_size, keep_mask))
    else:
        row_of = positions // IMG
        column_of = positions % IMG
        for down_step in (-1, 0, 1):
            for across_step in (-1, 0, 1):
                keep_mask = (
                    (row_of + down_step >= 0)
                    & (row_of + down_step < IMG)
                    & (column_of + across_step >= 0)
                    & (column_of + across_step < IMG)
                ).astype(jnp.float32)
                tap_list.append((down_step * IMG + across_step, keep_mask))
    return tap_list


def plane_shift(values, offset, keep_mask):
    margin = IMG + 1
    cell_count = values.shape[-1]
    widths = [(0, 0)] * (values.ndim - 1) + [(margin, margin)]
    padded = jnp.pad(values, widths)
    shifted = lax.slice_in_dim(
        padded, margin + offset, margin + offset + cell_count, axis=values.ndim - 1
    )
    return shifted * keep_mask.astype(values.dtype)


def expand(source, row_count, tap_list):
    pieces = []
    for depth_index in range(3):
        layer_rows = lax.slice_in_dim(source, depth_index, depth_index + row_count, axis=1)
        for offset, keep_mask in tap_list:
            pieces.append(plane_shift(layer_rows, offset, keep_mask))
    return jnp.concatenate(pieces, axis=0)


def collapse(hidden, w_out, row_count, tap_list):
    partial_value = jnp.einsum("to,ozn->tzn", w_out, hidden, preferred_element_type=jnp.float32)
    summed = jnp.zeros((row_count, hidden.shape[2]), jnp.float32)
    tap_number = 0
    for depth_index in range(3):
        for offset, keep_mask in tap_list:
            layer_rows = lax.slice_in_dim(
                partial_value[tap_number], depth_index, depth_index + row_count, axis=0
            )
            summed = summed + plane_shift(layer_rows, offset, keep_mask)
            tap_number = tap_number + 1
    return summed


def first_layer(extended, row_count, net_mode, weights):
    dual_in, dual_out, primal_in, primal_out = weights
    hidden_count = primal_in.shape[0]
    pad_count = hidden_count - dual_in.shape[0]
    cell_count = extended.shape[2]

    def first_dual_branch(source):
        columns = expand(source, row_count, plane_taps(0))
        hidden = jax.nn.relu(
            jnp.einsum("ok,kzn->ozn", dual_in, columns, preferred_element_type=jnp.float32)
        ).astype(jnp.bfloat16)
        return jnp.pad(hidden, ((0, pad_count), (0, 0), (0, 0)))

    def first_primal_branch(source):
        columns = expand(source[:2], row_count, plane_taps(1))
        return jax.nn.relu(
            jnp.einsum("ok,kzn->ozn", primal_in, columns, preferred_element_type=jnp.float32)
        ).astype(jnp.bfloat16)

    def first_skip_branch(source):
        return jnp.zeros((hidden_count, row_count, cell_count), jnp.bfloat16)

    return lax.switch(
        net_mode, [first_dual_branch, first_primal_branch, first_skip_branch], extended
    )


def second_layer(hidden, row_count, net_mode, weights):
    dual_in, dual_out, primal_in, primal_out = weights
    dual_count = dual_in.shape[0]
    cell_count = hidden.shape[2]

    def second_dual_branch(source):
        return collapse(source[:dual_count], dual_out, row_count, plane_taps(0))

    def second_primal_branch(source):
        return collapse(source, primal_out, row_count, plane_taps(1))

    def second_skip_branch(source):
        return jnp.zeros((row_count, cell_count), jnp.float32)

    return lax.switch(
        net_mode, [second_dual_branch, second_primal_branch, second_skip_branch], hidden
    )


def network_update(channels, net_mode, weights):
    row_count = channels.shape[1]
    extended = padded_2(channels, (("gz", 1),), 1)
    hidden = first_layer(extended, row_count, net_mode, weights)
    hidden = padded_2(as_sent(hidden), (("gz", 1),), 1).astype(hidden.dtype)
    return second_layer(hidden, row_count, net_mode, weights)


def band_local(padded, shifts, projector, band_mode, row_count):
    cell_count = padded.shape[1]
    groups = shifts.shape[0]
    group_width = cell_count // groups

    def forward(source):
        starts = row_count - 1 + shifts
        windows = jax.vmap(
            lambda start_row: lax.dynamic_slice_in_dim(source, start_row, row_count + 2, 0)
        )(starts)
        by_group = jnp.zeros((row_count, groups, group_width), jnp.float32)
        for tap_row in range(3):
            window_rows = lax.slice_in_dim(windows, tap_row, tap_row + row_count, axis=1)
            by_group = by_group + jnp.einsum(
                "gzp,pgc->zgc",
                window_rows,
                projector[tap_row].reshape(cell_count, groups, group_width),
                preferred_element_type=jnp.float32,
            )
        return by_group.reshape(row_count, cell_count)

    def adjoint(source):
        starts = row_count - 1 - shifts
        grouped = source.reshape(source.shape[0], groups, group_width)
        windows = jax.vmap(
            lambda column, start_row: lax.dynamic_slice_in_dim(column, start_row, row_count + 2, 0),
            in_axes=(1, 0),
        )(grouped, starts)
        summed = jnp.zeros((row_count, cell_count), jnp.float32)
        for tap_row in range(3):
            window_rows = lax.slice_in_dim(windows, 2 - tap_row, 2 - tap_row + row_count, axis=1)
            summed = summed + jnp.einsum(
                "gzc,pgc->zp",
                window_rows,
                projector[tap_row].reshape(cell_count, groups, group_width),
                preferred_element_type=jnp.float32,
            )
        return summed

    def band_skip_branch(source):
        return jnp.zeros((row_count, cell_count), jnp.float32)

    return lax.switch(band_mode, [forward, adjoint, band_skip_branch], padded)


def band_apply(values, shifts, projector, band_mode):
    row_count = values.shape[0]
    rounded = values.astype(jnp.bfloat16)
    padded = padded_2(rounded, (("gz", 0),), row_count)
    return band_local(padded, shifts, projector, band_mode, row_count)


def per_device(
    start_volume, sinogram, offsets, projector, dual_in, dual_out, primal_in, primal_out
):
    row_count = start_volume.shape[1]
    cell_count = start_volume.shape[2]
    segment_index = lax.axis_index("segment")
    weights = (dual_in, dual_out, primal_in, primal_out)
    empty_rows = jnp.zeros((row_count, cell_count), jnp.float32)
    current = start_volume[segment_index]
    dual_state = jnp.zeros_like(current)
    dual_mode = jnp.int32(0)
    primal_mode = jnp.int32(1)
    for rounds in range(ITERS):
        forward = band_apply(current, offsets[segment_index], projector, jnp.int32(0))
        channels = jnp.stack([dual_state, forward, sinogram[segment_index]]).astype(jnp.bfloat16)
        dual_state = dual_state + network_update(channels, dual_mode, weights)
        backward = band_apply(dual_state, offsets[segment_index], projector, jnp.int32(1))
        channels = jnp.stack([current, backward, empty_rows]).astype(jnp.bfloat16)
        current = current + network_update(channels, primal_mode, weights)
    return current[None]


def solution(mesh):
    in_specs = (P(None, "gz", None), P(None, "gz", None), P(), P(), P(), P(), P(), P())
    out_specs = P("segment", "gz", None)
    return jax.shard_map(
        per_device, mesh=mesh, in_specs=in_specs, out_specs=out_specs, check_vma=False
    )
```

profile of v0, /device:TPU:1, one launch (start us, length us, event | category | flops | bytes accessed | tf_op | source)
XLA Modules:
  0.0 217.8 jit_solution(9987832536005113659)
XLA Ops:
  1.5 4.6 %collective-permute-start = (bf16[16,1024]{1,0:T(8,128)(2,1)S(1)}, bf16[16,1024]{1,0:T(8,128)(2,1)S(1)}, u32[]{:S(2)}, u32[]{:S(2)}) collective-permute-start(bf16[16,1024]{1,0:T(8,128)(2,1)S(1)} %get-tuple-element.83), channel_id=1, source_target_pairs={{0,1},{1,2},{2,3},{3,4},{4,5},{5,6},{6,7},{8,9},{9,10},{10,11},{11... | collective-permute-start | bytes 98312 | tf_op jit(solution)/shard_map/ppermute | solution.py:19
  10.5 5.5 %fusion.281 = (bf16[1,1024,1024]{2,1,0:T(8,128)(2,1)}, bf16[1,1024,1024]{2,1,0:T(8,128)(2,1)S(1)}, bf16[1,1024,1024]{2,1,0:T(8,128)(2,1)}) fusion(bf16[3,1024,1024]{2,1,0:T(8,128)(2,1)} %param.11), kind=kLoop, calls=%fused_computation.554 | loop fusion | bytes 12582912 | tf_op jit(solution)/shard_map/cond/branch_0_fun/slice | solution.py:162
  16.8 3.9 %copy.108 = bf16[1,1024,1024]{1,2,0:T(8,128)(2,1)} copy(bf16[1,1024,1024]{2,1,0:T(8,128)(2,1)} %get-tuple-element.87) | data formatting | bytes 4194304
  20.7 2.6 %copy.109 = bf16[1,1024,1024]{1,2,0:T(8,128)(2,1)} copy(bf16[1,1024,1024]{2,1,0:T(8,128)(2,1)S(1)} %get-tuple-element.86) | data formatting | bytes 4194304
  23.3 2.9 %copy.110 = bf16[1,1024,1024]{1,2,0:T(8,128)(2,1)S(1)} copy(bf16[1,1024,1024]{2,1,0:T(8,128)(2,1)} %get-tuple-element.85) | data formatting | bytes 4194304
  26.3 10.2 %while.2 = (s32[]{:T(128)}, bf16[48,1024]{1,0:T(8,128)(2,1)S(1)}, s32[8,2]{0,1:T(2,128)S(1)}, bf16[8,18,1024]{2,1,0:T(8,128)(2,1)S(1)}, s32[]{:T(128)}) while((s32[]{:T(128)}, bf16[48,1024]{1,0:T(8,128)(2,1)S(1)}, s32[8,2]{0,1:T(2,128)S(1)}, bf16[8,18,1024]{2,1,0:T(8,128)(2,1)S(1)}, s32[]{:T(128)}) %tuple.197), condition=%wide.while_cond, body=%wide.while_body.sunk | while | flops 2 | bytes 98401 | solution.py:154
  41.2 3.6 %collective-permute-start.2 = (bf16[3,1,1024]{2,0,1:T(4,128)(2,1)S(1)}, bf16[3,1,1024]{2,0,1:T(4,128)(2,1)S(1)}, u32[]{:S(2)}, u32[]{:S(2)}) collective-permute-start(bf16[3,1,1024]{2,0,1:T(4,128)(2,1)S(1)} %get-tuple-element.189), channel_id=1, source_target_pairs={{0,1},{1,2},{2,3},{3,4},{4,5},{5,6},{6,7},{8,9},{9,10},{10,11},{11... | collective-permute-start | bytes 18440 | tf_op jit(solution)/shard_map/ppermute | solution.py:19
  47.4 2.4 %collective-permute-done.3 = bf16[3,1,1024]{2,0,1:T(4,128)(2,1)S(1)} collective-permute-done((bf16[3,1,1024]{2,0,1:T(4,128)(2,1)S(1)}, bf16[3,1,1024]{2,0,1:T(4,128)(2,1)S(1)}, u32[]{:S(2)}, u32[]{:S(2)}) %collective-permute-start.3) | collective-permute-done | bytes 6176 | tf_op jit(solution)/shard_map/ppermute | solution.py:21
  52.7 11.1 %concatenate.82 = bf16[27,16,1024]{2,0,1:T(8,128)(2,1)S(1)} concatenate(bf16[3,16,1024]{2,0,1:T(4,128)(2,1)} %get-tuple-element.193, bf16[3,16,1024]{2,0,1:T(4,128)(2,1)} %get-tuple-element.168, bf16[3,16,1024]{2,0,1:T(4,128)(2,1)} %get-tuple-element.192, bf16[3,16,1024]{2,0,1:T(4,128)(2,1)} %get-tuple-element.258, bf16[3,16,1024]{2,0,1:T(4,128)(2,1)} %get-tuple-element.79, ...), dimensions={0} | concatenate | bytes 1769472 | tf_op jit(solution)/shard_map/cond/branch_0_fun/concatenate | solution.py:75
  69.7 3.5 %collective-permute-done.5 = bf16[64,1,1024]{2,0,1:T(8,128)(2,1)S(1)} collective-permute-done((bf16[64,1,1024]{2,0,1:T(8,128)(2,1)S(1)}, bf16[64,1,1024]{2,0,1:T(8,128)(2,1)S(1)}, u32[]{:S(2)}, u32[]{:S(2)}) %collective-permute-start.5) | collective-permute-done | bytes 131104 | tf_op jit(solution)/shard_map/ppermute | solution.py:21
  79.4 2.7 %collective-permute-done.7 = bf16[16,1024]{1,0:T(8,128)(2,1)S(1)} collective-permute-done((bf16[16,1024]{1,0:T(8,128)(2,1)S(1)}, bf16[16,1024]{1,0:T(8,128)(2,1)S(1)}, u32[]{:S(2)}, u32[]{:S(2)}) %collective-permute-start.7) | collective-permute-done | bytes 32800 | tf_op jit(solution)/shard_map/ppermute | solution.py:21
  88.0 2.6 %collective-permute-start.9 = (bf16[3,1,1024]{2,0,1:T(4,128)(2,1)S(1)}, bf16[3,1,1024]{2,0,1:T(4,128)(2,1)S(1)}, u32[]{:S(2)}, u32[]{:S(2)}) collective-permute-start(bf16[3,1,1024]{2,0,1:T(4,128)(2,1)S(1)} %get-tuple-element.184), channel_id=1, source_target_pairs={{1,0},{2,1},{3,2},{4,3},{5,4},{6,5},{7,6},{9,8},{10,9},{11,10},{12... | collective-permute-start | bytes 18440 | tf_op jit(solution)/shard_map/ppermute | solution.py:21
  98.2 11.2 %concatenate.88 = bf16[54,16,1024]{2,0,1:T(8,128)(2,1)} concatenate(bf16[2,16,1024]{2,0,1:T(2,128)(2,1)} %get-tuple-element.241, bf16[2,16,1024]{2,0,1:T(2,128)(2,1)} %get-tuple-element.240, bf16[2,16,1024]{2,0,1:T(2,128)(2,1)} %get-tuple-element.235, bf16[2,16,1024]{2,0,1:T(2,128)(2,1)} %get-tuple-element.236, bf16[2,16,1024]{2,0,1:T(2,128)(2,1)S(1)} %get-tuple-element.166, ...), dimensions={0} | concatenate | bytes 3538944 | tf_op jit(solution)/shard_map/cond/branch_1_fun/concatenate | solution.py:75
  116.2 3.8 %collective-permute-done.11 = bf16[64,1,1024]{2,0,1:T(8,128)(2,1)S(1)} collective-permute-done((bf16[64,1,1024]{2,0,1:T(8,128)(2,1)S(1)}, bf16[64,1,1024]{2,0,1:T(8,128)(2,1)S(1)}, u32[]{:S(2)}, u32[]{:S(2)}) %collective-permute-start.11) | collective-permute-done | bytes 131104 | tf_op jit(solution)/shard_map/ppermute | solution.py:21
  128.1 2.8 %collective-permute-done.13 = bf16[16,1024]{1,0:T(8,128)(2,1)S(1)} collective-permute-done((bf16[16,1024]{1,0:T(8,128)(2,1)S(1)}, bf16[16,1024]{1,0:T(8,128)(2,1)S(1)}, u32[]{:S(2)}, u32[]{:S(2)}) %collective-permute-start.13) | collective-permute-done | bytes 32800 | tf_op jit(solution)/shard_map/ppermute | solution.py:21
  130.9 10.3 %while.3 = (s32[]{:T(128)}, bf16[48,1024]{1,0:T(8,128)(2,1)S(1)}, s32[8,2]{0,1:T(2,128)S(1)}, bf16[8,18,1024]{2,1,0:T(8,128)(2,1)S(1)}, s32[]{:T(128)}) while((s32[]{:T(128)}, bf16[48,1024]{1,0:T(8,128)(2,1)S(1)}, s32[8,2]{0,1:T(2,128)S(1)}, bf16[8,18,1024]{2,1,0:T(8,128)(2,1)S(1)}, s32[]{:T(128)}) %tuple.203), condition=%wide.while_cond.1, body=%wide.while_body.1.sunk | while | flops 2 | bytes 98401 | solution.py:154
  147.9 2.6 %collective-permute-start.15 = (bf16[3,1,1024]{2,0,1:T(4,128)(2,1)S(1)}, bf16[3,1,1024]{2,0,1:T(4,128)(2,1)S(1)}, u32[]{:S(2)}, u32[]{:S(2)}) collective-permute-start(bf16[3,1,1024]{2,0,1:T(4,128)(2,1)S(1)} %get-tuple-element.178), channel_id=1, source_target_pairs={{1,0},{2,1},{3,2},{4,3},{5,4},{6,5},{7,6},{9,8},{10,9},{11,10},{12... | collective-permute-start | bytes 18440 | tf_op jit(solution)/shard_map/ppermute | solution.py:21
  155.7 11.1 %concatenate.93 = bf16[27,16,1024]{2,0,1:T(8,128)(2,1)S(1)} concatenate(bf16[3,16,1024]{2,0,1:T(4,128)(2,1)} %get-tuple-element.183, bf16[3,16,1024]{2,0,1:T(4,128)(2,1)} %get-tuple-element.164, bf16[3,16,1024]{2,0,1:T(4,128)(2,1)} %get-tuple-element.182, bf16[3,16,1024]{2,0,1:T(4,128)(2,1)} %get-tuple-element.262, bf16[3,16,1024]{2,0,1:T(4,128)(2,1)} %get-tuple-element.63, ...), dimensions={0} | concatenate | bytes 1769472 | tf_op jit(solution)/shard_map/cond/branch_0_fun/concatenate | solution.py:75
  172.7 3.6 %collective-permute-done.17 = bf16[64,1,1024]{2,0,1:T(8,128)(2,1)S(1)} collective-permute-done((bf16[64,1,1024]{2,0,1:T(8,128)(2,1)S(1)}, bf16[64,1,1024]{2,0,1:T(8,128)(2,1)S(1)}, u32[]{:S(2)}, u32[]{:S(2)}) %collective-permute-start.17) | collective-permute-done | bytes 131104 | tf_op jit(solution)/shard_map/ppermute | solution.py:21
  182.1 2.7 %collective-permute-done.19 = bf16[16,1024]{1,0:T(8,128)(2,1)S(1)} collective-permute-done((bf16[16,1024]{1,0:T(8,128)(2,1)S(1)}, bf16[16,1024]{1,0:T(8,128)(2,1)S(1)}, u32[]{:S(2)}, u32[]{:S(2)}) %collective-permute-start.19) | collective-permute-done | bytes 32800 | tf_op jit(solution)/shard_map/ppermute | solution.py:21
  193.2 2.5 %collective-permute-done.21 = bf16[3,1,1024]{2,0,1:T(4,128)(2,1)S(1)} collective-permute-done((bf16[3,1,1024]{2,0,1:T(4,128)(2,1)S(1)}, bf16[3,1,1024]{2,0,1:T(4,128)(2,1)S(1)}, u32[]{:S(2)}, u32[]{:S(2)}) %collective-permute-start.21) | collective-permute-done | bytes 6176 | tf_op jit(solution)/shard_map/ppermute | solution.py:21
  199.6 5.2 %concatenate.98 = bf16[54,16,1024]{2,0,1:T(8,128)(2,1)S(1)} concatenate(bf16[2,16,1024]{2,0,1:T(2,128)(2,1)} %get-tuple-element.217, bf16[2,16,1024]{2,0,1:T(2,128)(2,1)S(1)} %get-tuple-element.216, bf16[2,16,1024]{2,0,1:T(2,128)(2,1)S(1)} %get-tuple-element.211, bf16[2,16,1024]{2,0,1:T(2,128)(2,1)S(1)} %get-tuple-element.212, bf16[2,16,1024]{2,0,1:T(2,128)(2,1)S(1)} %get-tuple-element.162, ...), dimensions={0} | concatenate | bytes 3538944 | tf_op jit(solution)/shard_map/cond/branch_1_fun/concatenate | solution.py:75
  207.6 2.6 %collective-permute-start.23 = (bf16[64,1,1024]{2,0,1:T(8,128)(2,1)S(1)}, bf16[64,1,1024]{2,0,1:T(8,128)(2,1)S(1)}, u32[]{:S(2)}, u32[]{:S(2)}) collective-permute-start(bf16[64,1,1024]{2,0,1:T(8,128)(2,1)S(1)} %get-tuple-element.140), channel_id=1, source_target_pairs={{1,0},{2,1},{3,2},{4,3},{5,4},{6,5},{7,6},{9,8},{10,9},{11,10},{12... | collective-permute-start | bytes 393224 | tf_op jit(solution)/shard_map/ppermute | solution.py:21
  210.3 3.6 %collective-permute-done.23 = bf16[64,1,1024]{2,0,1:T(8,128)(2,1)S(1)} collective-permute-done((bf16[64,1,1024]{2,0,1:T(8,128)(2,1)S(1)}, bf16[64,1,1024]{2,0,1:T(8,128)(2,1)S(1)}, u32[]{:S(2)}, u32[]{:S(2)}) %collective-permute-start.23) | collective-permute-done | bytes 131104 | tf_op jit(solution)/shard_map/ppermute | solution.py:21
  (333 shorter events, 118.4 us)
Async XLA Ops:
  1.5 24.7 %collective-permute-start = (bf16[16,1024]{1,0:T(8,128)(2,1)S(1)}, bf16[16,1024]{1,0:T(8,128)(2,1)S(1)}, u32[]{:S(2)}, u32[]{:S(2)}) collective-permute-start(bf16[16,1024]{1,0:T(8,128)(2,1)S(1)} %get-tuple-element.83), channel_id=1, source_target_pairs={{0,1},{1,2},{2,3},{3,4},{4,5},{5,6},{6,7},{8,9},{9,10},{10,11},{11... | collective-permute-start | bytes 98312 | tf_op jit(solution)/shard_map/ppermute | solution.py:19
  6.1 20.1 %collective-permute-start.1 = (bf16[16,1024]{1,0:T(8,128)(2,1)S(1)}, bf16[16,1024]{1,0:T(8,128)(2,1)S(1)}, u32[]{:S(2)}, u32[]{:S(2)}) collective-permute-start(bf16[16,1024]{1,0:T(8,128)(2,1)S(1)} %get-tuple-element.83), channel_id=1, source_target_pairs={{1,0},{2,1},{3,2},{4,3},{5,4},{6,5},{7,6},{9,8},{10,9},{11,10},{12... | collective-permute-start | bytes 98312 | tf_op jit(solution)/shard_map/ppermute | solution.py:21
  41.2 6.2 %collective-permute-start.2 = (bf16[3,1,1024]{2,0,1:T(4,128)(2,1)S(1)}, bf16[3,1,1024]{2,0,1:T(4,128)(2,1)S(1)}, u32[]{:S(2)}, u32[]{:S(2)}) collective-permute-start(bf16[3,1,1024]{2,0,1:T(4,128)(2,1)S(1)} %get-tuple-element.189), channel_id=1, source_target_pairs={{0,1},{1,2},{2,3},{3,4},{4,5},{5,6},{6,7},{8,9},{9,10},{10,11},{11... | collective-permute-start | bytes 18440 | tf_op jit(solution)/shard_map/ppermute | solution.py:19
  44.8 5.0 %collective-permute-start.3 = (bf16[3,1,1024]{2,0,1:T(4,128)(2,1)S(1)}, bf16[3,1,1024]{2,0,1:T(4,128)(2,1)S(1)}, u32[]{:S(2)}, u32[]{:S(2)}) collective-permute-start(bf16[3,1,1024]{2,0,1:T(4,128)(2,1)S(1)} %get-tuple-element.188), channel_id=1, source_target_pairs={{1,0},{2,1},{3,2},{4,3},{5,4},{6,5},{7,6},{9,8},{10,9},{11,10},{12... | collective-permute-start | bytes 18440 | tf_op jit(solution)/shard_map/ppermute | solution.py:21
  65.0 4.7 %collective-permute-start.4 = (bf16[64,1,1024]{2,0,1:T(8,128)(2,1)S(1)}, bf16[64,1,1024]{2,0,1:T(8,128)(2,1)S(1)}, u32[]{:S(2)}, u32[]{:S(2)}) collective-permute-start(bf16[64,1,1024]{2,0,1:T(8,128)(2,1)S(1)} %get-tuple-element.154), channel_id=1, source_target_pairs={{0,1},{1,2},{2,3},{3,4},{4,5},{5,6},{6,7},{8,9},{9,10},{10,11},{11... | collective-permute-start | bytes 393224 | tf_op jit(solution)/shard_map/ppermute | solution.py:19
  66.9 6.3 %collective-permute-start.5 = (bf16[64,1,1024]{2,0,1:T(8,128)(2,1)S(1)}, bf16[64,1,1024]{2,0,1:T(8,128)(2,1)S(1)}, u32[]{:S(2)}, u32[]{:S(2)}) collective-permute-start(bf16[64,1,1024]{2,0,1:T(8,128)(2,1)S(1)} %get-tuple-element.155), channel_id=1, source_target_pairs={{1,0},{2,1},{3,2},{4,3},{5,4},{6,5},{7,6},{9,8},{10,9},{11,10},{12... | collective-permute-start | bytes 393224 | tf_op jit(solution)/shard_map/ppermute | solution.py:21
  74.9 4.5 %collective-permute-start.6 = (bf16[16,1024]{1,0:T(8,128)(2,1)S(1)}, bf16[16,1024]{1,0:T(8,128)(2,1)S(1)}, u32[]{:S(2)}, u32[]{:S(2)}) collective-permute-start(bf16[16,1024]{1,0:T(8,128)(2,1)S(1)} %get-tuple-element.75), channel_id=1, source_target_pairs={{0,1},{1,2},{2,3},{3,4},{4,5},{5,6},{6,7},{8,9},{9,10},{10,11},{11... | collective-permute-start | bytes 98312 | tf_op jit(solution)/shard_map/ppermute | solution.py:19
  76.8 5.2 %collective-permute-start.7 = (bf16[16,1024]{1,0:T(8,128)(2,1)S(1)}, bf16[16,1024]{1,0:T(8,128)(2,1)S(1)}, u32[]{:S(2)}, u32[]{:S(2)}) collective-permute-start(bf16[16,1024]{1,0:T(8,128)(2,1)S(1)} %get-tuple-element.75), channel_id=1, source_target_pairs={{1,0},{2,1},{3,2},{4,3},{5,4},{6,5},{7,6},{9,8},{10,9},{11,10},{12... | collective-permute-start | bytes 98312 | tf_op jit(solution)/shard_map/ppermute | solution.py:21
  86.1 4.5 %collective-permute-start.8 = (bf16[3,1,1024]{2,0,1:T(4,128)(2,1)S(1)}, bf16[3,1,1024]{2,0,1:T(4,128)(2,1)S(1)}, u32[]{:S(2)}, u32[]{:S(2)}) collective-permute-start(bf16[3,1,1024]{2,0,1:T(4,128)(2,1)S(1)} %get-tuple-element.185), channel_id=1, source_target_pairs={{0,1},{1,2},{2,3},{3,4},{4,5},{5,6},{6,7},{8,9},{9,10},{10,11},{11... | collective-permute-start | bytes 18440 | tf_op jit(solution)/shard_map/ppermute | solution.py:19
  88.0 5.0 %collective-permute-start.9 = (bf16[3,1,1024]{2,0,1:T(4,128)(2,1)S(1)}, bf16[3,1,1024]{2,0,1:T(4,128)(2,1)S(1)}, u32[]{:S(2)}, u32[]{:S(2)}) collective-permute-start(bf16[3,1,1024]{2,0,1:T(4,128)(2,1)S(1)} %get-tuple-element.184), channel_id=1, source_target_pairs={{1,0},{2,1},{3,2},{4,3},{5,4},{6,5},{7,6},{9,8},{10,9},{11,10},{12... | collective-permute-start | bytes 18440 | tf_op jit(solution)/shard_map/ppermute | solution.py:21
  111.8 4.4 %collective-permute-start.10 = (bf16[64,1,1024]{2,0,1:T(8,128)(2,1)S(1)}, bf16[64,1,1024]{2,0,1:T(8,128)(2,1)S(1)}, u32[]{:S(2)}, u32[]{:S(2)}) collective-permute-start(bf16[64,1,1024]{2,0,1:T(8,128)(2,1)S(1)} %get-tuple-element.141), channel_id=1, source_target_pairs={{0,1},{1,2},{2,3},{3,4},{4,5},{5,6},{6,7},{8,9},{9,10},{10,11},{11... | collective-permute-start | bytes 393224 | tf_op jit(solution)/shard_map/ppermute | solution.py:19
  113.7 6.3 %collective-permute-start.11 = (bf16[64,1,1024]{2,0,1:T(8,128)(2,1)S(1)}, bf16[64,1,1024]{2,0,1:T(8,128)(2,1)S(1)}, u32[]{:S(2)}, u32[]{:S(2)}) collective-permute-start(bf16[64,1,1024]{2,0,1:T(8,128)(2,1)S(1)} %get-tuple-element.142), channel_id=1, source_target_pairs={{1,0},{2,1},{3,2},{4,3},{5,4},{6,5},{7,6},{9,8},{10,9},{11,10},{12... | collective-permute-start | bytes 393224 | tf_op jit(solution)/shard_map/ppermute | solution.py:21
  123.7 4.4 %collective-permute-start.12 = (bf16[16,1024]{1,0:T(8,128)(2,1)S(1)}, bf16[16,1024]{1,0:T(8,128)(2,1)S(1)}, u32[]{:S(2)}, u32[]{:S(2)}) collective-permute-start(bf16[16,1024]{1,0:T(8,128)(2,1)S(1)} %get-tuple-element.67), channel_id=1, source_target_pairs={{0,1},{1,2},{2,3},{3,4},{4,5},{5,6},{6,7},{8,9},{9,10},{10,11},{11... | collective-permute-start | bytes 98312 | tf_op jit(solution)/shard_map/ppermute | solution.py:19
  125.6 5.2 %collective-permute-start.13 = (bf16[16,1024]{1,0:T(8,128)(2,1)S(1)}, bf16[16,1024]{1,0:T(8,128)(2,1)S(1)}, u32[]{:S(2)}, u32[]{:S(2)}) collective-permute-start(bf16[16,1024]{1,0:T(8,128)(2,1)S(1)} %get-tuple-element.67), channel_id=1, source_target_pairs={{1,0},{2,1},{3,2},{4,3},{5,4},{6,5},{7,6},{9,8},{10,9},{11,10},{12... | collective-permute-start | bytes 98312 | tf_op jit(solution)/shard_map/ppermute | solution.py:21
  146.0 4.6 %collective-permute-start.14 = (bf16[3,1,1024]{2,0,1:T(4,128)(2,1)S(1)}, bf16[3,1,1024]{2,0,1:T(4,128)(2,1)S(1)}, u32[]{:S(2)}, u32[]{:S(2)}) collective-permute-start(bf16[3,1,1024]{2,0,1:T(4,128)(2,1)S(1)} %get-tuple-element.179), channel_id=1, source_target_pairs={{0,1},{1,2},{2,3},{3,4},{4,5},{5,6},{6,7},{8,9},{9,10},{10,11},{11... | collective-permute-start | bytes 18440 | tf_op jit(solution)/shard_map/ppermute | solution.py:19
  147.9 5.0 %collective-permute-start.15 = (bf16[3,1,1024]{2,0,1:T(4,128)(2,1)S(1)}, bf16[3,1,1024]{2,0,1:T(4,128)(2,1)S(1)}, u32[]{:S(2)}, u32[]{:S(2)}) collective-permute-start(bf16[3,1,1024]{2,0,1:T(4,128)(2,1)S(1)} %get-tuple-element.178), channel_id=1, source_target_pairs={{1,0},{2,1},{3,2},{4,3},{5,4},{6,5},{7,6},{9,8},{10,9},{11,10},{12... | collective-permute-start | bytes 18440 | tf_op jit(solution)/shard_map/ppermute | solution.py:21
  168.1 4.6 %collective-permute-start.16 = (bf16[64,1,1024]{2,0,1:T(8,128)(2,1)S(1)}, bf16[64,1,1024]{2,0,1:T(8,128)(2,1)S(1)}, u32[]{:S(2)}, u32[]{:S(2)}) collective-permute-start(bf16[64,1,1024]{2,0,1:T(8,128)(2,1)S(1)} %get-tuple-element.152), channel_id=1, source_target_pairs={{0,1},{1,2},{2,3},{3,4},{4,5},{5,6},{6,7},{8,9},{9,10},{10,11},{11... | collective-permute-start | bytes 393224 | tf_op jit(solution)/shard_map/ppermute | solution.py:19
  170.0 6.3 %collective-permute-start.17 = (bf16[64,1,1024]{2,0,1:T(8,128)(2,1)S(1)}, bf16[64,1,1024]{2,0,1:T(8,128)(2,1)S(1)}, u32[]{:S(2)}, u32[]{:S(2)}) collective-permute-start(bf16[64,1,1024]{2,0,1:T(8,128)(2,1)S(1)} %get-tuple-element.153), channel_id=1, source_target_pairs={{1,0},{2,1},{3,2},{4,3},{5,4},{6,5},{7,6},{9,8},{10,9},{11,10},{12... | collective-permute-start | bytes 393224 | tf_op jit(solution)/shard_map/ppermute | solution.py:21
  177.7 4.4 %collective-permute-start.18 = (bf16[16,1024]{1,0:T(8,128)(2,1)S(1)}, bf16[16,1024]{1,0:T(8,128)(2,1)S(1)}, u32[]{:S(2)}, u32[]{:S(2)}) collective-permute-start(bf16[16,1024]{1,0:T(8,128)(2,1)S(1)} %fusion.125), channel_id=1, source_target_pairs={{0,1},{1,2},{2,3},{3,4},{4,5},{5,6},{6,7},{8,9},{9,10},{10,11},{11... | collective-permute-start | bytes 98312 | tf_op jit(solution)/shard_map/ppermute | solution.py:19
  179.6 5.2 %collective-permute-start.19 = (bf16[16,1024]{1,0:T(8,128)(2,1)S(1)}, bf16[16,1024]{1,0:T(8,128)(2,1)S(1)}, u32[]{:S(2)}, u32[]{:S(2)}) collective-permute-start(bf16[16,1024]{1,0:T(8,128)(2,1)S(1)} %fusion.125), channel_id=1, source_target_pairs={{1,0},{2,1},{3,2},{4,3},{5,4},{6,5},{7,6},{9,8},{10,9},{11,10},{12... | collective-permute-start | bytes 98312 | tf_op jit(solution)/shard_map/ppermute | solution.py:21
  188.9 4.3 %collective-permute-start.20 = (bf16[3,1,1024]{2,0,1:T(4,128)(2,1)S(1)}, bf16[3,1,1024]{2,0,1:T(4,128)(2,1)S(1)}, u32[]{:S(2)}, u32[]{:S(2)}) collective-permute-start(bf16[3,1,1024]{2,0,1:T(4,128)(2,1)S(1)} %get-tuple-element.175), channel_id=1, source_target_pairs={{0,1},{1,2},{2,3},{3,4},{4,5},{5,6},{6,7},{8,9},{9,10},{10,11},{11... | collective-permute-start | bytes 18440 | tf_op jit(solution)/shard_map/ppermute | solution.py:19
  190.8 5.0 %collective-permute-start.21 = (bf16[3,1,1024]{2,0,1:T(4,128)(2,1)S(1)}, bf16[3,1,1024]{2,0,1:T(4,128)(2,1)S(1)}, u32[]{:S(2)}, u32[]{:S(2)}) collective-permute-start(bf16[3,1,1024]{2,0,1:T(4,128)(2,1)S(1)} %get-tuple-element.174), channel_id=1, source_target_pairs={{1,0},{2,1},{3,2},{4,3},{5,4},{6,5},{7,6},{9,8},{10,9},{11,10},{12... | collective-permute-start | bytes 18440 | tf_op jit(solution)/shard_map/ppermute | solution.py:21
  205.7 4.6 %collective-permute-start.22 = (bf16[64,1,1024]{2,0,1:T(8,128)(2,1)S(1)}, bf16[64,1,1024]{2,0,1:T(8,128)(2,1)S(1)}, u32[]{:S(2)}, u32[]{:S(2)}) collective-permute-start(bf16[64,1,1024]{2,0,1:T(8,128)(2,1)S(1)} %get-tuple-element.139), channel_id=1, source_target_pairs={{0,1},{1,2},{2,3},{3,4},{4,5},{5,6},{6,7},{8,9},{9,10},{10,11},{11... | collective-permute-start | bytes 393224 | tf_op jit(solution)/shard_map/ppermute | solution.py:19
  207.6 6.3 %collective-permute-start.23 = (bf16[64,1,1024]{2,0,1:T(8,128)(2,1)S(1)}, bf16[64,1,1024]{2,0,1:T(8,128)(2,1)S(1)}, u32[]{:S(2)}, u32[]{:S(2)}) collective-permute-start(bf16[64,1,1024]{2,0,1:T(8,128)(2,1)S(1)} %get-tuple-element.140), channel_id=1, source_target_pairs={{1,0},{2,1},{3,2},{4,3},{5,4},{6,5},{7,6},{9,8},{10,9},{11,10},{12... | collective-permute-start | bytes 393224 | tf_op jit(solution)/shard_map/ppermute | solution.py:21
  (60 other events, 570.2 us)
where the time goes:
time: 221 us; the launch traced here: 218 us
  local copies, waits for them, and re-layouts  81.4 us (37%)
  starting transfers between devices  56 us (25%)
  waiting for transfers between devices  32.4 us (15%)
  other arithmetic  25.5 us (12%)
  matrix products  20.5 us (9%)
    concatenate x4, local copies, waits for them, and re-layouts, expand(): return jnp.concatenate(pieces, axis=0)  38.7 us
    ppermute x12, waiting for transfers between devices, padded_2(): lax.ppermute(head, axis, [((i + 1) % count, i) for i in range(ends)])  32.4 us
    ppermute x12, starting transfers between devices, padded_2(): lax.ppermute(head, axis, [((i + 1) % count, i) for i in range(ends)])  28.5 us
    ppermute x12, starting transfers between devices, padded_2(): lax.ppermute(tail, axis, [(i, (i + 1) % count) for i in range(ends)])  27.5 us
    gather x48, local copies, waits for them, and re-layouts  20.1 us
    mul x16, other arithmetic, plane_shift(): return shifted * keep_mask.astype(values.dtype)  16.4 us
    unnamed x159, local copies, waits for them, and re-layouts  11.3 us
    dot_general x6, matrix products, forward(): jnp.einsum('gzp,pgc->zgc', window_rows, projector[tap_row].reshape(cell_c...  7.44 us
  transfers between devices with their start and end apart: 24, of which 11 were waited for; matrix products, arithmetic and copies ran while one was open for 9% of the time, Pallas kernels for 0%

commit v1 on v0

v1 whole, which is shorter than its diff:
```python
import functools

import jax
import jax.numpy as jnp
import numpy as np
from jax import lax
from jax.experimental import pallas as pl
from jax.experimental.pallas import tpu as pltpu
from jax.sharding import PartitionSpec as P

IMG = 32
LANES = 128
BLOCK = 8
PAD = 16
HALO_BLOCKS = 5

DUAL_SHIFTS = (-1, 0, 1)
PRIMAL_SHIFTS = tuple((dy, dx) for dy in (-1, 0, 1) for dx in (-1, 0, 1))


def first_structure(shift_count, channels, width):
    main = shift_count * channels * BLOCK
    table = np.zeros((3 * shift_count * channels, BLOCK * width), np.float32)
    for z in range(BLOCK):
        for dz in range(3):
            row = z + dz - 1
            for s in range(shift_count):
                for c in range(channels):
                    if row < 0:
                        column = main + s * BLOCK + 2 * c
                    elif row >= BLOCK:
                        column = main + s * BLOCK + 2 * c + 1
                    else:
                        column = (s * channels + c) * BLOCK + row
                    table[(dz * shift_count + s) * channels + c, z * width + column] = 1
    return table


def second_structure(shift_count, tap_width):
    table = np.zeros((shift_count * 2 * BLOCK, BLOCK * tap_width), np.float32)
    for z in range(BLOCK):
        for dz in range(3):
            row = z - dz + 1
            for s in range(shift_count):
                if row < 0:
                    place = s * 2 * BLOCK + BLOCK + BLOCK - 1
                elif row >= BLOCK:
                    place = s * 2 * BLOCK + BLOCK
                else:
                    place = s * 2 * BLOCK + row
                table[place, z * tap_width + dz * shift_count + s] = 1
    return table


def place_structure(hidden):
    return np.tile(np.eye(hidden, dtype=np.float32), (1, BLOCK))


def dot(a, b):
    return jnp.dot(a, b, preferred_element_type=jnp.float32)


def lanes():
    return lax.broadcasted_iota(jnp.int32, (BLOCK, LANES), 1)


def rows_of():
    return lax.broadcasted_iota(jnp.int32, (BLOCK, LANES), 0)


def shift_dual(tiles, step):
    if step == 0:
        return tiles
    lane = lanes()
    keep = (lane + step >= 0) & (lane + step < LANES)
    return [jnp.where(keep, pltpu.roll(t, (-step) % LANES, 1), 0.0) for t in tiles]


def shift_primal(tiles, step):
    dy, dx = step
    offset = dy * IMG + dx
    if offset == 0:
        return tiles
    lane = lanes()
    column = lane % IMG
    inside = (column + dx >= 0) & (column + dx < IMG)
    near = inside & (lane + offset >= 0) & (lane + offset < LANES)
    far = inside & ((lane + offset < 0) | (lane + offset >= LANES))
    rolled = [pltpu.roll(t, (-offset) % LANES, 1) for t in tiles]
    side = 1 if offset > 0 else -1
    out = []
    for j in range(len(tiles)):
        value = jnp.where(near, rolled[j], 0.0)
        if 0 <= j + side < len(tiles):
            value = jnp.where(far, rolled[j + side], value)
        out.append(value)
    return out


def kernel(sizes, info, own_start, *refs):
    window, tiles = sizes
    pieces = refs[:window]
    (projector, dual_in, dual_out, primal_in, primal_out, d_first, d_second, d_place,
     p_first, p_second, p_place, out, f_s, sino_s, t_s, a_s, h_s, b_s, x_s, y_s, lhs_s,
     w1d, w2d, w1p, w2p, spread) = refs[window:]
    row_count = own_start.shape[0]
    total = window * row_count
    blocks = total // BLOCK
    cells = tiles * LANES
    own = info[0]
    own_block = own // BLOCK

    def offset_of(view):
        return info[1 + window + view]

    def build(first, w_in, w1, second, place, w_out, w2, width, tap_width):
        hidden = w_in.shape[0]
        wide = dot(w_in[...], first[...])
        for z in range(BLOCK):
            w1[z * hidden:(z + 1) * hidden, :] = wide[:, z * width:(z + 1) * width].astype(jnp.bfloat16)
        across = dot(w_out[...], place[...])
        total_hidden = BLOCK * hidden
        lane = lax.broadcasted_iota(jnp.int32, across.shape, 1)
        taps = w_out.shape[0]
        spread[...] = jnp.zeros(spread.shape, spread.dtype)
        for z in range(BLOCK):
            spread[z * tap_width:z * tap_width + taps, 0:total_hidden] = jnp.where(
                lane // hidden == z, across, 0.0)
        w2[...] = dot(second[...], spread[0:BLOCK * tap_width, 0:total_hidden].astype(jnp.bfloat16)
                      ).astype(jnp.bfloat16)

    build(d_first, dual_in, w1d, d_second, d_place, dual_out, w2d, 128, 16)
    build(p_first, primal_in, w1p, p_second, p_place, primal_out, w2p, 256, 32)

    zero_rows = jnp.zeros((tiles, PAD, LANES), jnp.float32)
    for field in (f_s, sino_s, t_s, a_s):
        field[:, 0:PAD, :] = zero_rows
        field[:, PAD + total:PAD + total + PAD, :] = zero_rows
    h_s[...] = jnp.zeros(h_s.shape, jnp.float32)
    b_s[...] = jnp.zeros(b_s.shape, jnp.float32)
    x_s[...] = jnp.zeros(x_s.shape, jnp.bfloat16)
    for i, piece in enumerate(pieces):
        at = pl.multiple_of(info[1 + i] + PAD, BLOCK)
        for j in range(tiles):
            cut = slice(j * LANES, (j + 1) * LANES)
            f_s[j, pl.ds(at, row_count), :] = piece[0, :, cut].astype(jnp.float32)
            sino_s[j, pl.ds(at, row_count), :] = piece[1, :, cut].astype(jnp.float32)
    for j in range(tiles):
        f_s[j, pl.ds(pl.multiple_of(own + PAD, BLOCK), row_count), :] = own_start[:, j * LANES:(j + 1) * LANES]

    def forward(first_row, count, z_first, z_count):
        for k in range(3):
            for j in range(tiles):
                lhs_s[0:count, k * cells + j * LANES:k * cells + (j + 1) * LANES] = f_s[
                    j, pl.ds(PAD + first_row + (k - 1), count), :].astype(jnp.bfloat16)
        for n in range(cells // 256):
            value = dot(lhs_s[0:count, :], projector[:, n * 256:(n + 1) * 256])
            for part in range(2):
                t_s[2 * n + part, pl.ds(pl.multiple_of(PAD + first_row, BLOCK), count), :] = value[
                    :, part * LANES:(part + 1) * LANES]
        for w in range(tiles):
            a_s[w, pl.ds(pl.multiple_of(PAD + z_first, BLOCK), z_count), :] = t_s[
                w, pl.ds(PAD + z_first + offset_of(w), z_count), :]

    def adjoint(z_first, count):
        for k in range(3):
            for w in range(tiles):
                lhs_s[0:count, k * cells + w * LANES:k * cells + (w + 1) * LANES] = h_s[
                    w, pl.ds(PAD + z_first - offset_of(w) - (k - 1), count), :].astype(jnp.bfloat16)
        for n in range(cells // 256):
            value = jnp.zeros((count, 256), jnp.float32)
            for k in range(3):
                value = value + lax.dot_general(
                    lhs_s[0:count, k * cells:(k + 1) * cells],
                    projector[k * cells + n * 256:k * cells + (n + 1) * 256, :],
                    (((1,), (1,)), ((), ())), preferred_element_type=jnp.float32)
            for part in range(2):
                b_s[2 * n + part, pl.ds(pl.multiple_of(PAD + z_first, BLOCK), count), :] = value[
                    :, part * LANES:(part + 1) * LANES]

    def network(fields, shifts, shift_tiles, w1, w2, block_first, block_count):
        count = len(shifts)
        depth = w1.shape[1]
        edge = jnp.zeros((2 * BLOCK * count, cells), jnp.float32)
        y_s[0, 0:2 * BLOCK * count, :] = edge
        y_s[block_count + 1, 0:2 * BLOCK * count, :] = edge

        @pl.loop(0, block_count)
        def _(i):
            base = pl.multiple_of(PAD + (block_first + i) * BLOCK, BLOCK)
            row = rows_of()
            mains = [[field[j, pl.ds(base, BLOCK), :] for j in range(tiles)] for field in fields]
            edges = []
            for j in range(tiles):
                value = jnp.zeros((BLOCK, LANES), jnp.float32)
                for c, field in enumerate(fields):
                    value = jnp.where(row == 2 * c, field[j, pl.ds(base - 1 - 2 * c, BLOCK), :], value)
                    value = jnp.where(row == 2 * c + 1, field[j, pl.ds(base + BLOCK - 1 - 2 * c, BLOCK), :], value)
                edges.append(value)
            arrays = [shift_tiles(main, s) for s in shifts for main in mains]
            arrays += [shift_tiles(edges, s) for s in shifts]
            if len(arrays) % 2:
                arrays.append([jnp.zeros((BLOCK, LANES), jnp.float32)] * tiles)
            for pair in range(len(arrays) // 2):
                for j in range(tiles):
                    x_s[pair * 16:(pair + 1) * 16, j * LANES:(j + 1) * LANES] = jnp.concatenate(
                        [arrays[2 * pair][j], arrays[2 * pair + 1][j]], axis=0).astype(jnp.bfloat16)
            for n in range(cells // 256):
                hidden = dot(w1[...], x_s[0:depth, n * 256:(n + 1) * 256]).astype(jnp.bfloat16)
                hidden = jnp.maximum(hidden, jnp.zeros_like(hidden))
                y_s[i + 1, 0:2 * BLOCK * count, n * 256:(n + 1) * 256] = dot(w2[...], hidden)

    def collapse(shifts, shift_tiles, slot):
        row = rows_of()
        total_value = None
        for s, step in enumerate(shifts):
            at = s * 2 * BLOCK
            merged = []
            for j in range(tiles):
                cut = slice(j * LANES, (j + 1) * LANES)
                outer = jnp.where(row == 0, y_s[slot - 1, at + BLOCK:at + 2 * BLOCK, cut], 0.0)
                outer = jnp.where(row == BLOCK - 1, y_s[slot + 1, at + BLOCK:at + 2 * BLOCK, cut], outer)
                merged.append(y_s[slot, at:at + BLOCK, cut] + outer)
            moved = shift_tiles(merged, step)
            total_value = moved if total_value is None else [a + b for a, b in zip(total_value, moved)]
        return total_value

    def update(field, shifts, shift_tiles, block_first, block_count):
        @pl.loop(0, block_count)
        def _(i):
            base = pl.multiple_of(PAD + (block_first + i) * BLOCK, BLOCK)
            for j, value in enumerate(collapse(shifts, shift_tiles, i + 1)):
                field[j, pl.ds(base, BLOCK), :] += value

    def block_range(reach, own_count=row_count // BLOCK):
        count = min(blocks, own_count + 2 * reach)
        return jnp.clip(own_block - reach, 0, blocks - count), count

    forward(jnp.int32(-BLOCK), total + 2 * BLOCK, 0, total)
    first, count = block_range(7)
    network((h_s, a_s, sino_s), DUAL_SHIFTS, shift_dual, w1d, w2d, first, count)
    update(h_s, DUAL_SHIFTS, shift_dual, first, count)
    first, count = block_range(5)
    adjoint(first * BLOCK, count * BLOCK)
    network((f_s, b_s), PRIMAL_SHIFTS, shift_primal, w1p, w2p, first, count)
    update(f_s, PRIMAL_SHIFTS, shift_primal, first, count)

    t_count = min(total + 2 * BLOCK, row_count + 10 * BLOCK)
    t_first = jnp.clip(own - 5 * BLOCK, -BLOCK, total + BLOCK - t_count)
    first, count = block_range(3)
    forward(t_first, t_count, first * BLOCK, count * BLOCK)
    network((h_s, a_s, sino_s), DUAL_SHIFTS, shift_dual, w1d, w2d, first, count)
    update(h_s, DUAL_SHIFTS, shift_dual, first, count)
    first, count = block_range(1)
    adjoint(first * BLOCK, count * BLOCK)
    network((f_s, b_s), PRIMAL_SHIFTS, shift_primal, w1p, w2p, first, count)
    for i in range(row_count // BLOCK):
        slot = own_block - first + i + 1
        base = pl.multiple_of(PAD + own + i * BLOCK, BLOCK)
        for j, value in enumerate(collapse(PRIMAL_SHIFTS, shift_primal, slot)):
            out[i * BLOCK:(i + 1) * BLOCK, j * LANES:(j + 1) * LANES] = f_s[j, pl.ds(base, BLOCK), :] + value


def gather(block, count):
    me = lax.axis_index("gz")
    window = min(count, 2 * HALO_BLOCKS + 1)
    if count & (count - 1) == 0 and count <= window:
        def swap(x, bits):
            return lax.ppermute(x, "gz", [(i, i ^ bits) for i in range(count)])

        held = {0: block}
        for bits in range(2, count, 4):
            held[bits] = swap(block, bits)
        for bits in range(4, count, 4):
            held[bits] = swap(block, bits)
        if count > 1:
            for bits in list(held):
                held[bits ^ 1] = swap(held[bits], 1)
        return [held[b] for b in sorted(held)], [me ^ b for b in sorted(held)], me
    first = jnp.clip(me - HALO_BLOCKS, 0, count - window)
    whole = lax.all_gather(block, "gz", axis=0)
    return [whole[first + j] for j in range(window)], list(range(window)), me - first


def per_device(
    start_volume, sinogram, offsets, projector, dual_in, dual_out, primal_in, primal_out
):
    row_count, cells = start_volume.shape[1:]
    tiles = cells // LANES
    segment = lax.axis_index("segment")
    own_start = start_volume[segment]
    block = jnp.stack([own_start, sinogram[segment]]).astype(jnp.bfloat16)
    pieces, places, own = gather(block, lax.axis_size("gz"))
    window = len(pieces)
    total = window * row_count
    info = jnp.concatenate([
        jnp.stack([jnp.int32(own)] + [jnp.int32(p) for p in places]) * row_count,
        offsets[segment],
    ])
    dual_hidden, primal_hidden = dual_in.shape[0], primal_in.shape[0]
    tables = [
        first_structure(3, 3, 128), second_structure(3, 16), place_structure(dual_hidden),
        first_structure(9, 2, 256), second_structure(9, 32), place_structure(primal_hidden),
    ]
    tables = [jnp.asarray(t, jnp.bfloat16) for t in tables]
    blocks = total // BLOCK
    padded = total + 2 * PAD
    field = pltpu.VMEM((tiles, padded, LANES), jnp.float32)
    whole = pl.BlockSpec(memory_space=pltpu.VMEM)
    operands = [own_start, *pieces, projector.reshape(-1, cells), dual_in, dual_out, primal_in,
                primal_out, *tables]
    result = pl.pallas_call(
        functools.partial(kernel, (window, tiles)),
        out_shape=jax.ShapeDtypeStruct((row_count, cells), jnp.float32),
        in_specs=[pl.BlockSpec(memory_space=pltpu.SMEM)] + [whole] * len(operands),
        out_specs=whole,
        scratch_shapes=[field] * 6 + [
            pltpu.VMEM((256, cells), jnp.bfloat16),
            pltpu.VMEM((min(blocks, 16) + 2, 144, cells), jnp.float32),
            pltpu.VMEM((total + 2 * BLOCK, 3 * cells), jnp.bfloat16),
            pltpu.VMEM((BLOCK * dual_hidden, 128), jnp.bfloat16),
            pltpu.VMEM((48, BLOCK * dual_hidden), jnp.bfloat16),
            pltpu.VMEM((BLOCK * primal_hidden, 256), jnp.bfloat16),
            pltpu.VMEM((144, BLOCK * primal_hidden), jnp.bfloat16),
            pltpu.VMEM((256, BLOCK * primal_hidden), jnp.float32),
        ],
        compiler_params=pltpu.CompilerParams(vmem_limit_bytes=48 * 1024 * 1024),
    )(info, *operands)
    return result[None]


def solution(mesh):
    in_specs = (P(None, "gz", None), P(None, "gz", None), P(), P(), P(), P(), P(), P())
    out_specs = P("segment", "gz", None)
    return jax.shard_map(
        per_device, mesh=mesh, in_specs=in_specs, out_specs=out_specs, check_vma=False
    )
```

time: 221 us -> 81.4 us (0.37); the launches traced: 218 us -> 80.6 us
  local copies, waits for them, and re-layouts: 81.4 us -> 9.65 us
  Pallas kernels: 0 us -> 60.6 us
  starting transfers between devices: 56 us -> 6.82 us
  waiting for transfers between devices: 32.4 us -> 3.36 us
  other arithmetic: 25.5 us -> 0.09 us
  matrix products: 20.5 us -> 0 us
    pallas_call x0 -> x1, Pallas kernels: none -> 60.6 us  [per_device(): pl.pallas_call(functools.partial(kernel, (window, tiles)), out_shape=jax....]
    ppermute x24 -> x7, starting transfers between devices: 56 us -> 6.82 us  [swap(): return lax.ppermute(x, 'gz', [(i, i ^ bits) for i in range(count)])]
    concatenate x5 -> x0, local copies, waits for them, and re-layouts: 38.7 us -> none  [the longest x4 38.7 us: expand(): return jnp.concatenate(pieces, axis=0)]
    ppermute x24 -> x7, waiting for transfers between devices: 32.4 us -> 3.36 us  [swap(): return lax.ppermute(x, 'gz', [(i, i ^ bits) for i in range(count)])]
    gather x50 -> x0, local copies, waits for them, and re-layouts: 21.5 us -> none
    dot_general x20 -> x0, matrix products: 20.5 us -> none  [the longest x6 7.44 us: forward(): jnp.einsum('gzp,pgc->zgc', window_rows, projector[tap_row].reshape(cell_c...]
    mul x16 -> x1, other arithmetic: 16.4 us -> 0.01 us  [per_device(): jnp.stack([jnp.int32(own)] + [jnp.int32(p) for p in places]) * row_count]
    slice x17 -> x0, local copies, waits for them, and re-layouts: 7.52 us -> none  [the longest x1 5.54 us: forward(): projector[tap_row].reshape(cell_count, groups, group_width)]
  transfers between devices with their start and end apart: 24 -> 7, of which waited for: 11 -> 3; matrix products, arithmetic and copies ran while one was open for 9% -> 2% of each run, Pallas kernels for 0% -> 0%
where the time goes in v1:
time: 81.4 us; the launch traced here: 80.6 us
  Pallas kernels  60.6 us (74%)
  local copies, waits for them, and re-layouts  9.65 us (12%)
  starting transfers between devices  6.82 us (8%)
  waiting for transfers between devices  3.36 us (4%)
    pallas_call x1, Pallas kernels, per_device(): pl.pallas_call(functools.partial(kernel, (window, tiles)), out_shape=jax....  60.6 us
    unnamed x21, local copies, waits for them, and re-layouts  7.81 us
    ppermute x7, starting transfers between devices, swap(): return lax.ppermute(x, 'gz', [(i, i ^ bits) for i in range(count)])  6.82 us
    ppermute x7, waiting for transfers between devices, swap(): return lax.ppermute(x, 'gz', [(i, i ^ bits) for i in range(count)])  3.36 us
  transfers between devices with their start and end apart: 7, of which 3 were waited for; matrix products, arithmetic and copies ran while one was open for 2% of the time, Pallas kernels for 0%

profile of v1, /device:TPU:1, one launch (start us, length us, event | category | flops | bytes accessed | tf_op | source)
XLA Modules:
  0.0 80.6 jit_solution(3165810890480174854)
XLA Ops:
  0.0 0.9 %dynamic-slice_convert_fusion = (bf16[1,16,1024]{2,1,0:T(8,128)(2,1)S(1)}, bf16[1,16,1024]{2,1,0:T(8,128)(2,1)S(1)}) fusion(f32[4,16,1024]{2,1,0:T(8,128)} %param.15, s32[]{:T(128)S(6)} %select_n.2, f32[4,16,1024]{2,1,0:T(8,128)} %param.14), kind=kLoop, calls=%fused_computation.1 | loop fusion | bytes 131076 | tf_op jit(solution)/shard_map/convert.1
  0.9 4.2 %collective-permute-start.5 = (bf16[2,16,1024]{2,1,0:T(8,128)(2,1)S(1)}, bf16[2,16,1024]{2,1,0:T(8,128)(2,1)S(1)}, u32[]{:S(2)}, u32[]{:S(2)}) collective-permute-start(bf16[2,16,1024]{2,1,0:T(8,128)(2,1)S(1)} %pad_maximum_fusion.refs_0_), channel_id=1, source_target_pairs={{0,6},{1,7},{2,4},{3,5},{4,2},{5,3},{6,0},{7,1},{8,14},{9,15},{10,... | collective-permute-start | bytes 196616 | tf_op jit(solution)/shard_map/ppermute | solution.py:269
  5.1 0.4 collective-permute-start.1
  5.5 1.2 %collective-permute-start = (bf16[2,16,1024]{2,1,0:T(8,128)(2,1)S(1)}, bf16[2,16,1024]{2,1,0:T(8,128)(2,1)S(1)}, u32[]{:S(2)}, u32[]{:S(2)}) collective-permute-start(bf16[2,16,1024]{2,1,0:T(8,128)(2,1)S(1)} %pad_maximum_fusion.refs_0_), channel_id=1, source_target_pairs={{0,1},{1,0},{2,3},{3,2},{4,5},{5,4},{6,7},{7,6},{8,9},{9,8},{10,11... | collective-permute-start | bytes 196616 | tf_op jit(solution)/shard_map/ppermute | solution.py:269
  6.7 0.8 %dynamic-slice_bitcast_fusion.own_start = f32[16,1024]{1,0:T(8,128)S(1)} fusion(f32[4,16,1024]{2,1,0:T(8,128)} %param.14, s32[]{:T(128)S(6)} %select_n.2), kind=kLoop, calls=%fused_computation.3 | loop fusion | bytes 131076 | tf_op jit(solution)/shard_map/squeeze | solution.py:291
  7.6 0.1 stack.40
  7.7 0.8 %copy.15.refs_11_ = bf16[64,54]{1,0:T(8,128)(2,1)S(1)} copy(bf16[64,54]{0,1:T(8,128)(2,1)} %param.20) | data formatting | bytes 13824 | tf_op args[6]
  8.5 0.2 collective-permute-start.6
  8.7 2.2 %collective-permute-done.3.refs_4_ = bf16[2,16,1024]{2,1,0:T(8,128)(2,1)S(1)} collective-permute-done((bf16[2,16,1024]{2,1,0:T(8,128)(2,1)S(1)}, bf16[2,16,1024]{2,1,0:T(8,128)(2,1)S(1)}, u32[]{:S(2)}, u32[]{:S(2)}) %collective-permute-start.3) | collective-permute-done | bytes 65568 | tf_op jit(solution)/shard_map/ppermute | solution.py:269
  10.8 0.8 %collective-permute-start.4 = (bf16[2,16,1024]{2,1,0:T(8,128)(2,1)S(1)}, bf16[2,16,1024]{2,1,0:T(8,128)(2,1)S(1)}, u32[]{:S(2)}, u32[]{:S(2)}) collective-permute-start(bf16[2,16,1024]{2,1,0:T(8,128)(2,1)S(1)} %collective-permute-done.3.refs_4_), channel_id=1, source_target_pairs={{0,1},{1,0},{2,3},{3,2},{4,5},{5,4},{6,7},{7,6},{8,9},{9,8},{10,11... | collective-permute-start | bytes 196616 | tf_op jit(solution)/shard_map/ppermute | solution.py:269
  11.7 0.0 collective-permute-start.2
  11.7 0.1 pad_add_fusion.info
  11.8 0.8 %collective-permute-done.4.refs_5_ = bf16[2,16,1024]{2,1,0:T(8,128)(2,1)S(1)} collective-permute-done((bf16[2,16,1024]{2,1,0:T(8,128)(2,1)S(1)}, bf16[2,16,1024]{2,1,0:T(8,128)(2,1)S(1)}, u32[]{:S(2)}, u32[]{:S(2)}) %collective-permute-start.4) | collective-permute-done | bytes 65568 | tf_op jit(solution)/shard_map/ppermute | solution.py:269
  12.6 0.4 collective-permute-done.2.refs_3_
  13.0 0.9 %copy-done.1 = bf16[54,2048]{1,0:T(8,128)(2,1)S(1)} copy-done((bf16[54,2048]{1,0:T(8,128)(2,1)S(1)}, bf16[54,2048]{1,0:T(8,128)(2,1)}, u32[]{:S(2)}) %copy-start.1) | copy-done | bytes 221208
  13.9 0.9 %copy-done.2 = bf16[144,256]{1,0:T(8,128)(2,1)S(1)} copy-done((bf16[144,256]{1,0:T(8,128)(2,1)S(1)}, bf16[144,256]{1,0:T(8,128)(2,1)}, u32[]{:S(2)}) %copy-start.2) | copy-done | bytes 73752
  14.8 0.8 %copy-done.3 = bf16[64,512]{1,0:T(8,128)(2,1)S(1)} copy-done((bf16[64,512]{1,0:T(8,128)(2,1)S(1)}, bf16[64,512]{1,0:T(8,128)(2,1)}, u32[]{:S(2)}) %copy-start.3) | copy-done | bytes 65560
  15.6 0.8 %copy-done.4 = bf16[27,1024]{1,0:T(8,128)(2,1)S(1)} copy-done((bf16[27,1024]{1,0:T(8,128)(2,1)S(1)}, bf16[27,1024]{1,0:T(8,128)(2,1)}, u32[]{:S(2)}) %copy-start.4) | copy-done | bytes 55320
  16.5 0.7 copy-done.5
  17.2 0.7 copy-done.6
  17.9 0.7 copy-done.7
  18.6 0.7 copy-done.8
  19.3 0.7 copy-done.9
  20.0 60.6 %shard_map.136 = f32[16,1024]{1,0:T(8,128)} custom-call(s32[17]{0:T(128)S(1)} %pad_add_fusion.info, f32[16,1024]{1,0:T(8,128)S(1)} %dynamic-slice_bitcast_fusion.own_start, bf16[2,16,1024]{2,1,0:T(8,128)(2,1)S(1)} %pad_maximum_fusion.refs_0_, bf16[2,16,1024]{2,1,0:T(8,128)(2,1)S(1)} %collective-permute-done.refs_1_, ...), custom_call_target="tpu_custom_call" | custom-call | tf_op jit(solution)/shard_map/pallas_call | solution.py:312
  (19 shorter events, 0.1 us)
Async XLA Ops:
  0.0 8.5 %copy-start = (s32[4,8]{1,0:T(4,128)S(1)}, s32[4,8]{1,0:T(4,128)}, u32[]{:S(2)}) copy-start(s32[4,8]{1,0:T(4,128)} %param.16) | copy-start | bytes 388
  0.9 7.6 %collective-permute-start.5 = (bf16[2,16,1024]{2,1,0:T(8,128)(2,1)S(1)}, bf16[2,16,1024]{2,1,0:T(8,128)(2,1)S(1)}, u32[]{:S(2)}, u32[]{:S(2)}) collective-permute-start(bf16[2,16,1024]{2,1,0:T(8,128)(2,1)S(1)} %pad_maximum_fusion.refs_0_), channel_id=1, source_target_pairs={{0,6},{1,7},{2,4},{3,5},{4,2},{5,3},{6,0},{7,1},{8,14},{9,15},{10,... | collective-permute-start | bytes 196616 | tf_op jit(solution)/shard_map/ppermute | solution.py:269
  5.1 5.7 %collective-permute-start.3 = (bf16[2,16,1024]{2,1,0:T(8,128)(2,1)S(1)}, bf16[2,16,1024]{2,1,0:T(8,128)(2,1)S(1)}, u32[]{:S(2)}, u32[]{:S(2)}) collective-permute-start(bf16[2,16,1024]{2,1,0:T(8,128)(2,1)S(1)} %pad_maximum_fusion.refs_0_), channel_id=1, source_target_pairs={{0,4},{1,5},{2,6},{3,7},{4,0},{5,1},{6,2},{7,3},{8,12},{9,13},{10,... | collective-permute-start | bytes 196616 | tf_op jit(solution)/shard_map/ppermute | solution.py:269
  5.1 6.6 %collective-permute-start.1 = (bf16[2,16,1024]{2,1,0:T(8,128)(2,1)S(1)}, bf16[2,16,1024]{2,1,0:T(8,128)(2,1)S(1)}, u32[]{:S(2)}, u32[]{:S(2)}) collective-permute-start(bf16[2,16,1024]{2,1,0:T(8,128)(2,1)S(1)} %pad_maximum_fusion.refs_0_), channel_id=1, source_target_pairs={{0,2},{1,3},{2,0},{3,1},{4,6},{5,7},{6,4},{7,5},{8,10},{9,11},{10,... | collective-permute-start | bytes 196616 | tf_op jit(solution)/shard_map/ppermute | solution.py:269
  5.5 6.3 %collective-permute-start = (bf16[2,16,1024]{2,1,0:T(8,128)(2,1)S(1)}, bf16[2,16,1024]{2,1,0:T(8,128)(2,1)S(1)}, u32[]{:S(2)}, u32[]{:S(2)}) collective-permute-start(bf16[2,16,1024]{2,1,0:T(8,128)(2,1)S(1)} %pad_maximum_fusion.refs_0_), channel_id=1, source_target_pairs={{0,1},{1,0},{2,3},{3,2},{4,5},{5,4},{6,7},{7,6},{8,9},{9,8},{10,11... | collective-permute-start | bytes 196616 | tf_op jit(solution)/shard_map/ppermute | solution.py:269
  8.5 3.3 %collective-permute-start.6 = (bf16[2,16,1024]{2,1,0:T(8,128)(2,1)S(1)}, bf16[2,16,1024]{2,1,0:T(8,128)(2,1)S(1)}, u32[]{:S(2)}, u32[]{:S(2)}) collective-permute-start(bf16[2,16,1024]{2,1,0:T(8,128)(2,1)S(1)} %collective-permute-done.5.refs_6_), channel_id=1, source_target_pairs={{0,1},{1,0},{2,3},{3,2},{4,5},{5,4},{6,7},{7,6},{8,9},{9,8},{10,11... | collective-permute-start | bytes 196616 | tf_op jit(solution)/shard_map/ppermute | solution.py:269
  10.8 1.7 %collective-permute-start.4 = (bf16[2,16,1024]{2,1,0:T(8,128)(2,1)S(1)}, bf16[2,16,1024]{2,1,0:T(8,128)(2,1)S(1)}, u32[]{:S(2)}, u32[]{:S(2)}) collective-permute-start(bf16[2,16,1024]{2,1,0:T(8,128)(2,1)S(1)} %collective-permute-done.3.refs_4_), channel_id=1, source_target_pairs={{0,1},{1,0},{2,3},{3,2},{4,5},{5,4},{6,7},{7,6},{8,9},{9,8},{10,11... | collective-permute-start | bytes 196616 | tf_op jit(solution)/shard_map/ppermute | solution.py:269
  11.7 1.3 %collective-permute-start.2 = (bf16[2,16,1024]{2,1,0:T(8,128)(2,1)S(1)}, bf16[2,16,1024]{2,1,0:T(8,128)(2,1)S(1)}, u32[]{:S(2)}, u32[]{:S(2)}) collective-permute-start(bf16[2,16,1024]{2,1,0:T(8,128)(2,1)S(1)} %collective-permute-done.1.refs_2_), channel_id=1, source_target_pairs={{0,1},{1,0},{2,3},{3,2},{4,5},{5,4},{6,7},{7,6},{8,9},{9,8},{10,11... | collective-permute-start | bytes 196616 | tf_op jit(solution)/shard_map/ppermute | solution.py:269
  13.0 0.9 %copy-start.1 = (bf16[54,2048]{1,0:T(8,128)(2,1)S(1)}, bf16[54,2048]{1,0:T(8,128)(2,1)}, u32[]{:S(2)}) copy-start(bf16[54,2048]{1,0:T(8,128)(2,1)} %constant.41.clone.refs_16_) | copy-start | bytes 663556
  13.9 0.9 %copy-start.2 = (bf16[144,256]{1,0:T(8,128)(2,1)S(1)}, bf16[144,256]{1,0:T(8,128)(2,1)}, u32[]{:S(2)}) copy-start(bf16[144,256]{1,0:T(8,128)(2,1)} %constant.42.clone.refs_17_) | copy-start | bytes 221188
  14.8 0.8 %copy-start.3 = (bf16[64,512]{1,0:T(8,128)(2,1)S(1)}, bf16[64,512]{1,0:T(8,128)(2,1)}, u32[]{:S(2)}) copy-start(bf16[64,512]{1,0:T(8,128)(2,1)} %constant.43.clone.refs_18_) | copy-start | bytes 196612
  15.6 0.8 %copy-start.4 = (bf16[27,1024]{1,0:T(8,128)(2,1)S(1)}, bf16[27,1024]{1,0:T(8,128)(2,1)}, u32[]{:S(2)}) copy-start(bf16[27,1024]{1,0:T(8,128)(2,1)} %constant.38.clone.refs_13_) | copy-start | bytes 165892
  16.5 0.7 copy-start.5
  17.2 0.7 copy-start.6
  17.9 0.7 copy-start.7
  18.6 0.7 copy-start.8
  19.3 0.7 copy-start.9

commit v2 on v1

--- a/solution.py
+++ b/solution.py
@@ -16,44 +16,6 @@
 
 DUAL_SHIFTS = (-1, 0, 1)
 PRIMAL_SHIFTS = tuple((dy, dx) for dy in (-1, 0, 1) for dx in (-1, 0, 1))
-
-
-def first_structure(shift_count, channels, width):
-    main = shift_count * channels * BLOCK
-    table = np.zeros((3 * shift_count * channels, BLOCK * width), np.float32)
-    for z in range(BLOCK):
-        for dz in range(3):
-            row = z + dz - 1
-            for s in range(shift_count):
-                for c in range(channels):
-                    if row < 0:
-                        column = main + s * BLOCK + 2 * c
-                    elif row >= BLOCK:
-                        column = main + s * BLOCK + 2 * c + 1
-                    else:
-                        column = (s * channels + c) * BLOCK + row
-                    table[(dz * shift_count + s) * channels + c, z * width + column] = 1
-    return table
-
-
-def second_structure(shift_count, tap_width):
-    table = np.zeros((shift_count * 2 * BLOCK, BLOCK * tap_width), np.float32)
-    for z in range(BLOCK):
-        for dz in range(3):
-            row = z - dz + 1
-            for s in range(shift_count):
-                if row < 0:
-                    place = s * 2 * BLOCK + BLOCK + BLOCK - 1
-                elif row >= BLOCK:
-                    place = s * 2 * BLOCK + BLOCK
-                else:
-                    place = s * 2 * BLOCK + row
-                table[place, z * tap_width + dz * shift_count + s] = 1
-    return table
-
-
-def place_structure(hidden):
-    return np.tile(np.eye(hidden, dtype=np.float32), (1, BLOCK))
 
 
 def dot(a, b):
@@ -97,12 +59,79 @@
     return out
 
 
+def iota(shape, dim):
+    return lax.broadcasted_iota(jnp.int32, shape, dim)
+
+
+def first_weights(w_in, taps, shift_count, channels, out):
+    width = out.shape[1]
+    hidden = w_in.shape[1]
+    arrays = shift_count * channels
+    main = arrays * BLOCK
+    column = iota((taps, width), 1)
+    row = iota((taps, width), 0)
+    place = column - main
+    outer = lax.bitwise_and(place, BLOCK - 1)
+    outer_tap = (place // BLOCK) * channels + outer // 2
+    used = (place >= 0) & (place < shift_count * BLOCK) & (outer < 2 * channels)
+    low = used & (outer % 2 == 0)
+    high = used & (outer % 2 == 1)
+    for z in range(BLOCK):
+        tap = (column % BLOCK - z + 1) * arrays + column // BLOCK
+        hit = (place < 0) & (row == tap)
+        if z == 0:
+            hit = hit | (low & (row == outer_tap))
+        if z == BLOCK - 1:
+            hit = hit | (high & (row == outer_tap + 2 * arrays))
+        table = jnp.where(hit, 1.0, 0.0).astype(jnp.bfloat16)
+        out[z * hidden:(z + 1) * hidden, :] = lax.dot_general(
+            w_in, table, (((0,), (0,)), ((), ())), preferred_element_type=jnp.float32
+        ).astype(jnp.bfloat16)
+
+
+def second_weights(w_out, hidden, shift_count, out):
+    taps = w_out.shape[0]
+    height, wide = out.shape
+    spread = jnp.where(iota((hidden, wide), 1) % hidden == iota((hidden, wide), 0), 1.0, 0.0)
+    across = dot(w_out, spread.astype(jnp.bfloat16)).astype(jnp.bfloat16)
+    place = iota((height, taps), 0)
+    tap = iota((height, taps), 1)
+    shift = place // (2 * BLOCK)
+    inner = (place // BLOCK) % 2 == 0
+    row = place % BLOCK
+    lane = iota((height, wide), 1) // hidden
+    total = jnp.zeros((height, wide), jnp.float32)
+    for z in range(BLOCK):
+        hit = inner & (tap == (z + 1 - row) * shift_count + shift)
+        if z == 0:
+            hit = hit | (~inner & (row == BLOCK - 1) & (tap == 2 * shift_count + shift))
+        if z == BLOCK - 1:
+            hit = hit | (~inner & (row == 0) & (tap == shift))
+        part = dot(jnp.where(hit, 1.0, 0.0).astype(jnp.bfloat16), across)
+        total = jnp.where(lane == z, part, total)
+    out[...] = total.astype(jnp.bfloat16)
+
+
+def prepare(sizes, weights, w1d, w2d, w1p, w2p):
+    (d_taps, d_hidden), (p_taps, p_hidden) = sizes
+    at = 0
+    parts = []
+    for rows, columns in ((d_taps, d_hidden), (d_taps // 3, d_hidden), (p_taps, p_hidden),
+                          (p_taps // 2, p_hidden)):
+        parts.append(weights[at:at + rows, 0:columns])
+        at += -(-rows // 16) * 16
+    first_weights(parts[0], d_taps, 3, 3, w1d)
+    second_weights(parts[1], d_hidden, 3, w2d)
+    first_weights(parts[2], p_taps, 9, 2, w1p)
+    second_weights(parts[3], p_hidden, 9, w2p)
+
+
 def kernel(sizes, info, own_start, *refs):
     window, tiles = sizes
     pieces = refs[:window]
-    (projector, dual_in, dual_out, primal_in, primal_out, d_first, d_second, d_place,
-     p_first, p_second, p_place, out, f_s, sino_s, t_s, a_s, h_s, b_s, x_s, y_s, lhs_s,
-     w1d, w2d, w1p, w2p, spread) = refs[window:]
+    (projector, w1d, w2d, w1p, w2p, out, f_s, sino_s, t_s, a_s, h_s, b_s, x_0, x_1, hidden_0, hidden_1,
+     y_s, lhs_s) = refs[window:]
+    x_refs, hidden_refs = (x_0, x_1), (hidden_0, hidden_1)
     row_count = own_start.shape[0]
     total = window * row_count
     blocks = total // BLOCK
@@ -113,32 +142,14 @@
     def offset_of(view):
         return info[1 + window + view]
 
-    def build(first, w_in, w1, second, place, w_out, w2, width, tap_width):
-        hidden = w_in.shape[0]
-        wide = dot(w_in[...], first[...])
-        for z in range(BLOCK):
-            w1[z * hidden:(z + 1) * hidden, :] = wide[:, z * width:(z + 1) * width].astype(jnp.bfloat16)
-        across = dot(w_out[...], place[...])
-        total_hidden = BLOCK * hidden
-        lane = lax.broadcasted_iota(jnp.int32, across.shape, 1)
-        taps = w_out.shape[0]
-        spread[...] = jnp.zeros(spread.shape, spread.dtype)
-        for z in range(BLOCK):
-            spread[z * tap_width:z * tap_width + taps, 0:total_hidden] = jnp.where(
-                lane // hidden == z, across, 0.0)
-        w2[...] = dot(second[...], spread[0:BLOCK * tap_width, 0:total_hidden].astype(jnp.bfloat16)
-                      ).astype(jnp.bfloat16)
-
-    build(d_first, dual_in, w1d, d_second, d_place, dual_out, w2d, 128, 16)
-    build(p_first, primal_in, w1p, p_second, p_place, primal_out, w2p, 256, 32)
-
     zero_rows = jnp.zeros((tiles, PAD, LANES), jnp.float32)
     for field in (f_s, sino_s, t_s, a_s):
         field[:, 0:PAD, :] = zero_rows
         field[:, PAD + total:PAD + total + PAD, :] = zero_rows
     h_s[...] = jnp.zeros(h_s.shape, jnp.float32)
     b_s[...] = jnp.zeros(b_s.shape, jnp.float32)
-    x_s[...] = jnp.zeros(x_s.shape, jnp.bfloat16)
+    for x in x_refs:
+        x[...] = jnp.zeros(x.shape, jnp.bfloat16)
     for i, piece in enumerate(pieces):
         at = pl.multiple_of(info[1 + i] + PAD, BLOCK)
         for j in range(tiles):
@@ -180,14 +191,13 @@
 
     def network(fields, shifts, shift_tiles, w1, w2, block_first, block_count):
         count = len(shifts)
-        depth = w1.shape[1]
-        edge = jnp.zeros((2 * BLOCK * count, cells), jnp.float32)
-        y_s[0, 0:2 * BLOCK * count, :] = edge
-        y_s[block_count + 1, 0:2 * BLOCK * count, :] = edge
-
-        @pl.loop(0, block_count)
-        def _(i):
-            base = pl.multiple_of(PAD + (block_first + i) * BLOCK, BLOCK)
+        hidden_rows, depth = w1.shape
+        out_rows = 2 * BLOCK * count
+        edge = jnp.zeros((out_rows, cells), jnp.float32)
+        y_s[0, 0:out_rows, :] = edge
+        y_s[block_count + 1, 0:out_rows, :] = edge
+
+        def build_taps(x, base):
             row = rows_of()
             mains = [[field[j, pl.ds(base, BLOCK), :] for j in range(tiles)] for field in fields]
             edges = []
@@ -203,12 +213,20 @@
                 arrays.append([jnp.zeros((BLOCK, LANES), jnp.float32)] * tiles)
             for pair in range(len(arrays) // 2):
                 for j in range(tiles):
-                    x_s[pair * 16:(pair + 1) * 16, j * LANES:(j + 1) * LANES] = jnp.concatenate(
+                    x[pair * 16:(pair + 1) * 16, j * LANES:(j + 1) * LANES] = jnp.concatenate(
                         [arrays[2 * pair][j], arrays[2 * pair + 1][j]], axis=0).astype(jnp.bfloat16)
-            for n in range(cells // 256):
-                hidden = dot(w1[...], x_s[0:depth, n * 256:(n + 1) * 256]).astype(jnp.bfloat16)
-                hidden = jnp.maximum(hidden, jnp.zeros_like(hidden))
-                y_s[i + 1, 0:2 * BLOCK * count, n * 256:(n + 1) * 256] = dot(w2[...], hidden)
+
+        group = len(x_refs)
+
+        @pl.loop(0, block_count // group)
+        def _(i):
+            for u in range(group):
+                build_taps(x_refs[u], pl.multiple_of(PAD + (block_first + i * group + u) * BLOCK, BLOCK))
+            for u in range(group):
+                hidden = dot(w1[...], x_refs[u][0:depth, :]).astype(jnp.bfloat16)
+                hidden_refs[u][0:hidden_rows, :] = jnp.maximum(hidden, jnp.zeros_like(hidden))
+            for u in range(group):
+                y_s[i * group + u + 1, 0:out_rows, :] = dot(w2[...], hidden_refs[u][0:hidden_rows, :])
 
     def collapse(shifts, shift_tiles, slot):
         row = rows_of()
@@ -236,8 +254,8 @@
         count = min(blocks, own_count + 2 * reach)
         return jnp.clip(own_block - reach, 0, blocks - count), count
 
+    first, count = block_range(7)
     forward(jnp.int32(-BLOCK), total + 2 * BLOCK, 0, total)
-    first, count = block_range(7)
     network((h_s, a_s, sino_s), DUAL_SHIFTS, shift_dual, w1d, w2d, first, count)
     update(h_s, DUAL_SHIFTS, shift_dual, first, count)
     first, count = block_range(5)
@@ -259,7 +277,6 @@
         base = pl.multiple_of(PAD + own + i * BLOCK, BLOCK)
         for j, value in enumerate(collapse(PRIMAL_SHIFTS, shift_primal, slot)):
             out[i * BLOCK:(i + 1) * BLOCK, j * LANES:(j + 1) * LANES] = f_s[j, pl.ds(base, BLOCK), :] + value
-
 
 def gather(block, count):
     me = lax.axis_index("gz")
@@ -298,17 +315,28 @@
         offsets[segment],
     ])
     dual_hidden, primal_hidden = dual_in.shape[0], primal_in.shape[0]
-    tables = [
-        first_structure(3, 3, 128), second_structure(3, 16), place_structure(dual_hidden),
-        first_structure(9, 2, 256), second_structure(9, 32), place_structure(primal_hidden),
-    ]
-    tables = [jnp.asarray(t, jnp.bfloat16) for t in tables]
+    parts = [dual_in.T, dual_out, primal_in.T, primal_out]
+    packed = jnp.concatenate([
+        jnp.pad(p, ((0, -p.shape[0] % 16), (0, primal_hidden - p.shape[1]))) for p in parts])
     blocks = total // BLOCK
     padded = total + 2 * PAD
     field = pltpu.VMEM((tiles, padded, LANES), jnp.float32)
     whole = pl.BlockSpec(memory_space=pltpu.VMEM)
-    operands = [own_start, *pieces, projector.reshape(-1, cells), dual_in, dual_out, primal_in,
-                primal_out, *tables]
+    flat = projector.reshape(-1, cells)
+    weights = pl.pallas_call(
+        functools.partial(prepare, (dual_in.shape[::-1], primal_in.shape[::-1])),
+        out_shape=[
+            jax.ShapeDtypeStruct(shape, jnp.bfloat16) for shape in (
+                (BLOCK * dual_hidden, 128), (48, BLOCK * dual_hidden),
+                (BLOCK * primal_hidden, 256), (144, BLOCK * primal_hidden))
+        ],
+        in_specs=[whole],
+        out_specs=[whole] * 4,
+        cost_estimate=pl.CostEstimate(flops=2_000_000_000, bytes_accessed=8_000_000, transcendentals=0),
+        compiler_params=pltpu.CompilerParams(vmem_limit_bytes=16 * 1024 * 1024),
+        name="prepare",
+    )(packed)
+    operands = [own_start, *pieces, flat, *weights]
     result = pl.pallas_call(
         functools.partial(kernel, (window, tiles)),
         out_shape=jax.ShapeDtypeStruct((row_count, cells), jnp.float32),
@@ -316,15 +344,14 @@
         out_specs=whole,
         scratch_shapes=[field] * 6 + [
             pltpu.VMEM((256, cells), jnp.bfloat16),
+            pltpu.VMEM((256, cells), jnp.bfloat16),
+            pltpu.VMEM((BLOCK * primal_hidden, cells), jnp.bfloat16),
+            pltpu.VMEM((BLOCK * primal_hidden, cells), jnp.bfloat16),
             pltpu.VMEM((min(blocks, 16) + 2, 144, cells), jnp.float32),
             pltpu.VMEM((total + 2 * BLOCK, 3 * cells), jnp.bfloat16),
-            pltpu.VMEM((BLOCK * dual_hidden, 128), jnp.bfloat16),
-            pltpu.VMEM((48, BLOCK * dual_hidden), jnp.bfloat16),
-            pltpu.VMEM((BLOCK * primal_hidden, 256), jnp.bfloat16),
-            pltpu.VMEM((144, BLOCK * primal_hidden), jnp.bfloat16),
-            pltpu.VMEM((256, BLOCK * primal_hidden), jnp.float32),
         ],
-        compiler_params=pltpu.CompilerParams(vmem_limit_bytes=48 * 1024 * 1024),
+        compiler_params=pltpu.CompilerParams(vmem_limit_bytes=32 * 1024 * 1024),
+        name="iterate",
     )(info, *operands)
     return result[None]
 

time: 81.4 us -> 42.3 us (0.52)
  Pallas kernels: 60.6 us -> 29.9 us
  local copies, waits for them, and re-layouts: 9.65 us -> 2.63 us
  waiting for transfers between devices: 3.36 us -> 1.63 us
  other arithmetic: 0.09 us -> 0.99 us
    pallas_call x1, Pallas kernels: 60.6 us -> 29 us  [per_device(): pl.pallas_call(functools.partial(kernel, (window, tiles)), out_shape=jax....]
    unnamed x21 -> x5, local copies, waits for them, and re-layouts: 7.81 us -> 0.79 us
    ppermute x7, waiting for transfers between devices: 3.36 us -> 1.63 us  [swap(): return lax.ppermute(x, 'gz', [(i, i ^ bits) for i in range(count)])]
    pallas_call x0 -> x1, Pallas kernels: none -> 0.92 us  [per_device(): pl.pallas_call(functools.partial(prepare, (dual_in.shape[::-1], primal_in...]
    concatenate x0 -> x1, other arithmetic: none -> 0.9 us  [per_device(): jnp.concatenate([jnp.pad(p, ((0, -p.shape[0] % 16), (0, primal_hidden - p...]
  transfers between devices with their start and end apart: 7 -> 7, of which waited for: 3 -> 3; matrix products, arithmetic and copies ran while one was open for 2% -> 6% of each run, Pallas kernels for 0% -> 2%
where the time goes in v2:
time: 42.3 us; the launch traced here: 41.9 us
  Pallas kernels  29.9 us (71%)
  starting transfers between devices  6.73 us (16%)
  local copies, waits for them, and re-layouts  2.63 us (6%)
  waiting for transfers between devices  1.63 us (4%)
  other arithmetic  0.99 us (2%)
    pallas_call x1, Pallas kernels, per_device(): pl.pallas_call(functools.partial(kernel, (window, tiles)), out_shape=jax....  29 us
    ppermute x7, starting transfers between devices, swap(): return lax.ppermute(x, 'gz', [(i, i ^ bits) for i in range(count)])  6.73 us
    ppermute x7, waiting for transfers between devices, swap(): return lax.ppermute(x, 'gz', [(i, i ^ bits) for i in range(count)])  1.63 us
    pallas_call x1, Pallas kernels, per_device(): pl.pallas_call(functools.partial(prepare, (dual_in.shape[::-1], primal_in...  0.92 us
    concatenate x1, other arithmetic, per_device(): jnp.concatenate([jnp.pad(p, ((0, -p.shape[0] % 16), (0, primal_hidden - p...  0.9 us
    another operation x1, local copies, waits for them, and re-layouts  0.89 us
  transfers between devices with their start and end apart: 7, of which 3 were waited for; matrix products, arithmetic and copies ran while one was open for 6% of the time, Pallas kernels for 2%

profile of v2, /device:TPU:1, one launch (start us, length us, event | category | flops | bytes accessed | tf_op | source)
XLA Modules:
  0.0 41.9 jit_solution(6970220010726943583)
XLA Ops:
  0.0 0.9 %dynamic-slice_convert_fusion = (bf16[1,16,1024]{2,1,0:T(8,128)(2,1)S(1)}, bf16[1,16,1024]{2,1,0:T(8,128)(2,1)S(1)}) fusion(f32[4,16,1024]{2,1,0:T(8,128)} %param.9, s32[]{:T(128)S(6)} %select_n.2, f32[4,16,1024]{2,1,0:T(8,128)} %param.8), kind=kLoop, calls=%fused_computation.13 | loop fusion | bytes 131076 | tf_op jit(solution)/shard_map/convert.1
  0.9 4.2 %collective-permute-start.5 = (bf16[2,16,1024]{2,1,0:T(8,128)(2,1)S(1)}, bf16[2,16,1024]{2,1,0:T(8,128)(2,1)S(1)}, u32[]{:S(2)}, u32[]{:S(2)}) collective-permute-start(bf16[2,16,1024]{2,1,0:T(8,128)(2,1)S(1)} %pad_maximum_fusion.refs_0_), channel_id=1, source_target_pairs={{0,6},{1,7},{2,4},{3,5},{4,2},{5,3},{6,0},{7,1},{8,14},{9,15},{10,... | collective-permute-start | bytes 196616 | tf_op jit(solution)/shard_map/ppermute | solution.py:286
  5.1 0.0 collective-permute-start.3
  5.1 0.4 collective-permute-start.1
  5.5 1.2 %collective-permute-start = (bf16[2,16,1024]{2,1,0:T(8,128)(2,1)S(1)}, bf16[2,16,1024]{2,1,0:T(8,128)(2,1)S(1)}, u32[]{:S(2)}, u32[]{:S(2)}) collective-permute-start(bf16[2,16,1024]{2,1,0:T(8,128)(2,1)S(1)} %pad_maximum_fusion.refs_0_), channel_id=1, source_target_pairs={{0,1},{1,0},{2,3},{3,2},{4,5},{5,4},{6,7},{7,6},{8,9},{9,8},{10,11... | collective-permute-start | bytes 196616 | tf_op jit(solution)/shard_map/ppermute | solution.py:286
  6.7 0.8 %dynamic-slice_bitcast_fusion.own_start = f32[16,1024]{1,0:T(8,128)S(1)} fusion(f32[4,16,1024]{2,1,0:T(8,128)} %param.8, s32[]{:T(128)S(6)} %select_n.2), kind=kLoop, calls=%fused_computation.15 | loop fusion | bytes 131076 | tf_op jit(solution)/shard_map/squeeze | solution.py:308
  7.6 0.1 stack.40
  7.7 0.8 %copy.9 = bf16[32,27]{0,1:T(8,128)(2,1)S(1)} copy(bf16[32,27]{1,0:T(8,128)(2,1)} %param.12) | data formatting | bytes 3456 | tf_op args[4]
  8.5 0.9 %fusion.7.weights = bf16[144,64]{1,0:T(8,128)(2,1)S(1)} fusion(bf16[27,64]{1,0:T(8,128)(2,1)} %param.15, bf16[54,64]{1,0:T(8,128)(2,1)} %bitcast.18, bf16[9,32]{1,0:T(8,128)(2,1)} %param.13, bf16[27,32]{1,0:T(8,128)(2,1)S(1)} %bitcast.17), kind=kLoop, calls=%fused_computation.17 | loop fusion | flops 184320 | bytes 31104 | tf_op jit(solution)/shard_map/concatenate | solution.py:319
  9.4 0.9 %prepare.1 = (bf16[256,128]{1,0:T(8,128)(2,1)S(1)}, bf16[48,256]{1,0:T(8,128)(2,1)S(1)}, bf16[512,256]{1,0:T(8,128)(2,1)S(1)}, bf16[144,512]{1,0:T(8,128)(2,1)S(1)}) custom-call(bf16[144,64]{1,0:T(8,128)(2,1)S(1)} %fusion.7.weights), custom_call_target="tpu_custom_call" | custom-call | flops 2000000000 | bytes 8000000 | tf_op jit(solution)/shard_map/prepare/pallas_call | solution.py:326
  10.3 0.0 copy-done
  10.3 0.0 collective-permute-done.5.refs_6_
  10.3 0.1 collective-permute-start.6
  10.4 0.4 %collective-permute-done.3.refs_4_ = bf16[2,16,1024]{2,1,0:T(8,128)(2,1)S(1)} collective-permute-done((bf16[2,16,1024]{2,1,0:T(8,128)(2,1)S(1)}, bf16[2,16,1024]{2,1,0:T(8,128)(2,1)S(1)}, u32[]{:S(2)}, u32[]{:S(2)}) %collective-permute-start.3) | collective-permute-done | bytes 65568 | tf_op jit(solution)/shard_map/ppermute | solution.py:286
  10.8 0.8 %collective-permute-start.4 = (bf16[2,16,1024]{2,1,0:T(8,128)(2,1)S(1)}, bf16[2,16,1024]{2,1,0:T(8,128)(2,1)S(1)}, u32[]{:S(2)}, u32[]{:S(2)}) collective-permute-start(bf16[2,16,1024]{2,1,0:T(8,128)(2,1)S(1)} %collective-permute-done.3.refs_4_), channel_id=1, source_target_pairs={{0,1},{1,0},{2,3},{3,2},{4,5},{5,4},{6,7},{7,6},{8,9},{9,8},{10,11... | collective-permute-start | bytes 196616 | tf_op jit(solution)/shard_map/ppermute | solution.py:286
  11.7 0.0 collective-permute-done.1.refs_2_
  11.7 0.0 collective-permute-start.2
  11.7 0.1 pad_add_fusion.info
  11.8 0.0 collective-permute-done.refs_1_
  11.8 0.0 collective-permute-done.6.refs_7_
  11.8 0.8 %collective-permute-done.4.refs_5_ = bf16[2,16,1024]{2,1,0:T(8,128)(2,1)S(1)} collective-permute-done((bf16[2,16,1024]{2,1,0:T(8,128)(2,1)S(1)}, bf16[2,16,1024]{2,1,0:T(8,128)(2,1)S(1)}, u32[]{:S(2)}, u32[]{:S(2)}) %collective-permute-start.4) | collective-permute-done | bytes 65568 | tf_op jit(solution)/shard_map/ppermute | solution.py:286
  12.6 0.4 collective-permute-done.2.refs_3_
  13.0 0.0 copy-done.1
  13.0 29.0 %iterate.1 = f32[16,1024]{1,0:T(8,128)} custom-call(s32[17]{0:T(128)S(1)} %pad_add_fusion.info, f32[16,1024]{1,0:T(8,128)S(1)} %dynamic-slice_bitcast_fusion.own_start, bf16[2,16,1024]{2,1,0:T(8,128)(2,1)S(1)} %pad_maximum_fusion.refs_0_, bf16[2,16,1024]{2,1,0:T(8,128)(2,1)S(1)} %collective-permute-done.refs_1_, ...), custom_call_target="tpu_custom_call" | custom-call | tf_op jit(solution)/shard_map/iterate/pallas_call | solution.py:340
  (5 shorter events, 0.0 us)
Async XLA Ops:
  0.0 10.3 %copy-start = (s32[4,8]{1,0:T(4,128)S(1)}, s32[4,8]{1,0:T(4,128)}, u32[]{:S(2)}) copy-start(s32[4,8]{1,0:T(4,128)} %param.10) | copy-start | bytes 388
  0.9 9.4 %collective-permute-start.5 = (bf16[2,16,1024]{2,1,0:T(8,128)(2,1)S(1)}, bf16[2,16,1024]{2,1,0:T(8,128)(2,1)S(1)}, u32[]{:S(2)}, u32[]{:S(2)}) collective-permute-start(bf16[2,16,1024]{2,1,0:T(8,128)(2,1)S(1)} %pad_maximum_fusion.refs_0_), channel_id=1, source_target_pairs={{0,6},{1,7},{2,4},{3,5},{4,2},{5,3},{6,0},{7,1},{8,14},{9,15},{10,... | collective-permute-start | bytes 196616 | tf_op jit(solution)/shard_map/ppermute | solution.py:286
  5.1 5.7 %collective-permute-start.3 = (bf16[2,16,1024]{2,1,0:T(8,128)(2,1)S(1)}, bf16[2,16,1024]{2,1,0:T(8,128)(2,1)S(1)}, u32[]{:S(2)}, u32[]{:S(2)}) collective-permute-start(bf16[2,16,1024]{2,1,0:T(8,128)(2,1)S(1)} %pad_maximum_fusion.refs_0_), channel_id=1, source_target_pairs={{0,4},{1,5},{2,6},{3,7},{4,0},{5,1},{6,2},{7,3},{8,12},{9,13},{10,... | collective-permute-start | bytes 196616 | tf_op jit(solution)/shard_map/ppermute | solution.py:286
  5.1 6.6 %collective-permute-start.1 = (bf16[2,16,1024]{2,1,0:T(8,128)(2,1)S(1)}, bf16[2,16,1024]{2,1,0:T(8,128)(2,1)S(1)}, u32[]{:S(2)}, u32[]{:S(2)}) collective-permute-start(bf16[2,16,1024]{2,1,0:T(8,128)(2,1)S(1)} %pad_maximum_fusion.refs_0_), channel_id=1, source_target_pairs={{0,2},{1,3},{2,0},{3,1},{4,6},{5,7},{6,4},{7,5},{8,10},{9,11},{10,... | collective-permute-start | bytes 196616 | tf_op jit(solution)/shard_map/ppermute | solution.py:286
  5.5 6.3 %collective-permute-start = (bf16[2,16,1024]{2,1,0:T(8,128)(2,1)S(1)}, bf16[2,16,1024]{2,1,0:T(8,128)(2,1)S(1)}, u32[]{:S(2)}, u32[]{:S(2)}) collective-permute-start(bf16[2,16,1024]{2,1,0:T(8,128)(2,1)S(1)} %pad_maximum_fusion.refs_0_), channel_id=1, source_target_pairs={{0,1},{1,0},{2,3},{3,2},{4,5},{5,4},{6,7},{7,6},{8,9},{9,8},{10,11... | collective-permute-start | bytes 196616 | tf_op jit(solution)/shard_map/ppermute | solution.py:286
  8.5 4.5 %copy-start.1 = (bf16[3,1024,1024]{2,1,0:T(8,128)(2,1)S(1)}, bf16[3,1024,1024]{2,1,0:T(8,128)(2,1)}, u32[]{:S(2)}) copy-start(bf16[3,1024,1024]{2,1,0:T(8,128)(2,1)} %param.11) | copy-start | bytes 18874372
  10.3 1.5 %collective-permute-start.6 = (bf16[2,16,1024]{2,1,0:T(8,128)(2,1)S(1)}, bf16[2,16,1024]{2,1,0:T(8,128)(2,1)S(1)}, u32[]{:S(2)}, u32[]{:S(2)}) collective-permute-start(bf16[2,16,1024]{2,1,0:T(8,128)(2,1)S(1)} %collective-permute-done.5.refs_6_), channel_id=1, source_target_pairs={{0,1},{1,0},{2,3},{3,2},{4,5},{5,4},{6,7},{7,6},{8,9},{9,8},{10,11... | collective-permute-start | bytes 196616 | tf_op jit(solution)/shard_map/ppermute | solution.py:286
  10.8 1.7 %collective-permute-start.4 = (bf16[2,16,1024]{2,1,0:T(8,128)(2,1)S(1)}, bf16[2,16,1024]{2,1,0:T(8,128)(2,1)S(1)}, u32[]{:S(2)}, u32[]{:S(2)}) collective-permute-start(bf16[2,16,1024]{2,1,0:T(8,128)(2,1)S(1)} %collective-permute-done.3.refs_4_), channel_id=1, source_target_pairs={{0,1},{1,0},{2,3},{3,2},{4,5},{5,4},{6,7},{7,6},{8,9},{9,8},{10,11... | collective-permute-start | bytes 196616 | tf_op jit(solution)/shard_map/ppermute | solution.py:286
  11.7 1.3 %collective-permute-start.2 = (bf16[2,16,1024]{2,1,0:T(8,128)(2,1)S(1)}, bf16[2,16,1024]{2,1,0:T(8,128)(2,1)S(1)}, u32[]{:S(2)}, u32[]{:S(2)}) collective-permute-start(bf16[2,16,1024]{2,1,0:T(8,128)(2,1)S(1)} %collective-permute-done.1.refs_2_), channel_id=1, source_target_pairs={{0,1},{1,0},{2,3},{3,2},{4,5},{5,4},{6,7},{7,6},{8,9},{9,8},{10,11... | collective-permute-start | bytes 196616 | tf_op jit(solution)/shard_map/ppermute | solution.py:286

commit v3 on v2

--- a/solution.py
+++ b/solution.py
@@ -13,9 +13,7 @@
 BLOCK = 8
 PAD = 16
 HALO_BLOCKS = 5
-
-DUAL_SHIFTS = (-1, 0, 1)
-PRIMAL_SHIFTS = tuple((dy, dx) for dy in (-1, 0, 1) for dx in (-1, 0, 1))
+LAG = 4
 
 
 def dot(a, b):
@@ -30,33 +28,62 @@
     return lax.broadcasted_iota(jnp.int32, (BLOCK, LANES), 0)
 
 
-def shift_dual(tiles, step):
-    if step == 0:
-        return tiles
+def masks_of():
     lane = lanes()
-    keep = (lane + step >= 0) & (lane + step < LANES)
-    return [jnp.where(keep, pltpu.roll(t, (-step) % LANES, 1), 0.0) for t in tiles]
-
-
-def shift_primal(tiles, step):
-    dy, dx = step
-    offset = dy * IMG + dx
-    if offset == 0:
-        return tiles
-    lane = lanes()
+    row = rows_of()
     column = lane % IMG
-    inside = (column + dx >= 0) & (column + dx < IMG)
-    near = inside & (lane + offset >= 0) & (lane + offset < LANES)
-    far = inside & ((lane + offset < 0) | (lane + offset >= LANES))
-    rolled = [pltpu.roll(t, (-offset) % LANES, 1) for t in tiles]
-    side = 1 if offset > 0 else -1
-    out = []
-    for j in range(len(tiles)):
-        value = jnp.where(near, rolled[j], 0.0)
-        if 0 <= j + side < len(tiles):
-            value = jnp.where(far, rolled[j + side], value)
-        out.append(value)
-    return out
+    return {
+        "view": {-1: lane > 0, 1: lane < LANES - 1},
+        "across": {-1: column > 0, 1: column < IMG - 1},
+        "down": {-1: lane >= IMG, 1: lane < LANES - IMG},
+        "rows": [row == r for r in range(BLOCK)],
+    }
+
+
+def shift_lanes(tiles, step, mask):
+    return [jnp.where(mask, pltpu.roll(t, (-step) % LANES, 1), 0.0) for t in tiles]
+
+
+def shift_down(tiles, dy, mask):
+    rolled = [pltpu.roll(t, (-dy * IMG) % LANES, 1) for t in tiles]
+    zero = jnp.zeros_like(tiles[0])
+    beyond = rolled[1:] + [zero] if dy > 0 else [zero] + rolled[:-1]
+    return [jnp.where(mask, near, far) for near, far in zip(rolled, beyond)]
+
+
+def dual_shifted(tiles, masks):
+    return [shift_lanes(tiles, -1, masks["view"][-1]), tiles, shift_lanes(tiles, 1, masks["view"][1])]
+
+
+def dual_sum(values, masks):
+    return add(add(shift_lanes(values(0), -1, masks["view"][-1]), values(1)),
+               shift_lanes(values(2), 1, masks["view"][1]))
+
+
+def primal_shifted(tiles, masks):
+    across = [shift_lanes(tiles, -1, masks["across"][-1]), tiles, shift_lanes(tiles, 1, masks["across"][1])]
+    return ([shift_down(t, -1, masks["down"][-1]) for t in across] + across
+            + [shift_down(t, 1, masks["down"][1]) for t in across])
+
+
+def primal_sum(values, masks):
+    total = None
+    for dy in (-1, 0, 1):
+        at = (dy + 1) * 3
+        part = add(add(shift_lanes(values(at), -1, masks["across"][-1]), values(at + 1)),
+                   shift_lanes(values(at + 2), 1, masks["across"][1]))
+        if dy:
+            part = shift_down(part, dy, masks["down"][dy])
+        total = part if total is None else add(total, part)
+    return total
+
+
+def add(a, b):
+    return [x + y for x, y in zip(a, b)]
+
+
+DUAL = (3, dual_shifted, dual_sum)
+PRIMAL = (9, primal_shifted, primal_sum)
 
 
 def iota(shape, dim):
@@ -129,9 +156,10 @@
 def kernel(sizes, info, own_start, *refs):
     window, tiles = sizes
     pieces = refs[:window]
-    (projector, w1d, w2d, w1p, w2p, out, f_s, sino_s, t_s, a_s, h_s, b_s, x_0, x_1, hidden_0, hidden_1,
-     y_s, lhs_s) = refs[window:]
-    x_refs, hidden_refs = (x_0, x_1), (hidden_0, hidden_1)
+    (projector, w1d, w2d, w1p, w2p, out, f_s, sino_s, t_s, a_s, h_s, b_s,
+     x_0, x_1, x_2, x_3, hidden_0, hidden_1, hidden_2, hidden_3, y_s, lhs_s,
+     across_s) = refs[window:]
+    x_refs, hidden_refs = ((x_0, x_1), (x_2, x_3)), ((hidden_0, hidden_1), (hidden_2, hidden_3))
     row_count = own_start.shape[0]
     total = window * row_count
     blocks = total // BLOCK
@@ -139,6 +167,8 @@
     own = info[0]
     own_block = own // BLOCK
 
+    masks = masks_of()
+
     def offset_of(view):
         return info[1 + window + view]
 
@@ -148,8 +178,6 @@
         field[:, PAD + total:PAD + total + PAD, :] = zero_rows
     h_s[...] = jnp.zeros(h_s.shape, jnp.float32)
     b_s[...] = jnp.zeros(b_s.shape, jnp.float32)
-    for x in x_refs:
-        x[...] = jnp.zeros(x.shape, jnp.bfloat16)
     for i, piece in enumerate(pieces):
         at = pl.multiple_of(info[1 + i] + PAD, BLOCK)
         for j in range(tiles):
@@ -173,42 +201,47 @@
             a_s[w, pl.ds(pl.multiple_of(PAD + z_first, BLOCK), z_count), :] = t_s[
                 w, pl.ds(PAD + z_first + offset_of(w), z_count), :]
 
+    def transpose_part(n):
+        columns = pl.ds(pl.multiple_of(n * 256, 256), 256)
+        for k in range(3):
+            rows = pl.ds(pl.multiple_of(k * cells + n * 256, 256), 256)
+            for m in range(cells // 256):
+                at = k * cells + m * 256
+                across_s[rows, m * 256:(m + 1) * 256] = projector[at:at + 256, columns].T
+
     def adjoint(z_first, count):
         for k in range(3):
             for w in range(tiles):
                 lhs_s[0:count, k * cells + w * LANES:k * cells + (w + 1) * LANES] = h_s[
                     w, pl.ds(PAD + z_first - offset_of(w) - (k - 1), count), :].astype(jnp.bfloat16)
         for n in range(cells // 256):
-            value = jnp.zeros((count, 256), jnp.float32)
-            for k in range(3):
-                value = value + lax.dot_general(
-                    lhs_s[0:count, k * cells:(k + 1) * cells],
-                    projector[k * cells + n * 256:k * cells + (n + 1) * 256, :],
-                    (((1,), (1,)), ((), ())), preferred_element_type=jnp.float32)
+            value = dot(lhs_s[0:count, :], across_s[:, n * 256:(n + 1) * 256])
             for part in range(2):
                 b_s[2 * n + part, pl.ds(pl.multiple_of(PAD + z_first, BLOCK), count), :] = value[
                     :, part * LANES:(part + 1) * LANES]
 
-    def network(fields, shifts, shift_tiles, w1, w2, block_first, block_count):
-        count = len(shifts)
+    def network(fields, plane, w1, w2, block_first, block_count, target=None, beside=None):
+        count, shifted, _ = plane
         hidden_rows, depth = w1.shape
         out_rows = 2 * BLOCK * count
+        group = len(x_refs[0])
+        groups = block_count // group
         edge = jnp.zeros((out_rows, cells), jnp.float32)
-        y_s[0, 0:out_rows, :] = edge
-        y_s[block_count + 1, 0:out_rows, :] = edge
-
-        def build_taps(x, base):
-            row = rows_of()
+        for slot in (LAG - 1, block_count + LAG):
+            y_s[slot, 0:out_rows, :] = edge
+
+        def build_taps(x, block):
+            base = pl.multiple_of(PAD + (block_first + block) * BLOCK, BLOCK)
             mains = [[field[j, pl.ds(base, BLOCK), :] for j in range(tiles)] for field in fields]
             edges = []
             for j in range(tiles):
                 value = jnp.zeros((BLOCK, LANES), jnp.float32)
                 for c, field in enumerate(fields):
-                    value = jnp.where(row == 2 * c, field[j, pl.ds(base - 1 - 2 * c, BLOCK), :], value)
-                    value = jnp.where(row == 2 * c + 1, field[j, pl.ds(base + BLOCK - 1 - 2 * c, BLOCK), :], value)
+                    value = jnp.where(masks["rows"][2 * c], field[j, pl.ds(base - 1 - 2 * c, BLOCK), :], value)
+                    value = jnp.where(masks["rows"][2 * c + 1], field[j, pl.ds(base + BLOCK - 1 - 2 * c, BLOCK), :], value)
                 edges.append(value)
-            arrays = [shift_tiles(main, s) for s in shifts for main in mains]
-            arrays += [shift_tiles(edges, s) for s in shifts]
+            moved = [shifted(main, masks) for main in mains]
+            arrays = [each[s] for s in range(count) for each in moved] + shifted(edges, masks)
             if len(arrays) % 2:
                 arrays.append([jnp.zeros((BLOCK, LANES), jnp.float32)] * tiles)
             for pair in range(len(arrays) // 2):
@@ -216,39 +249,50 @@
                     x[pair * 16:(pair + 1) * 16, j * LANES:(j + 1) * LANES] = jnp.concatenate(
                         [arrays[2 * pair][j], arrays[2 * pair + 1][j]], axis=0).astype(jnp.bfloat16)
 
-        group = len(x_refs)
-
-        @pl.loop(0, block_count // group)
+        def add_block(block, guarded):
+            value = collapse(plane, block + LAG)
+            at = jnp.maximum(block, 0) if guarded else block
+            base = pl.multiple_of(PAD + (block_first + at) * BLOCK, BLOCK)
+            for j in range(tiles):
+                part = jnp.where(block >= 0, value[j], 0.0) if guarded else value[j]
+                target[j, pl.ds(base, BLOCK), :] += part
+
+        for u in range(group):
+            build_taps(x_refs[0][u], u)
+
+        @pl.loop(0, groups // 2)
         def _(i):
-            for u in range(group):
-                build_taps(x_refs[u], pl.multiple_of(PAD + (block_first + i * group + u) * BLOCK, BLOCK))
-            for u in range(group):
-                hidden = dot(w1[...], x_refs[u][0:depth, :]).astype(jnp.bfloat16)
-                hidden_refs[u][0:hidden_rows, :] = jnp.maximum(hidden, jnp.zeros_like(hidden))
-            for u in range(group):
-                y_s[i * group + u + 1, 0:out_rows, :] = dot(w2[...], hidden_refs[u][0:hidden_rows, :])
-
-    def collapse(shifts, shift_tiles, slot):
-        row = rows_of()
-        total_value = None
-        for s, step in enumerate(shifts):
+            for phase in range(2):
+                now = (2 * i + phase) * group
+                after = jnp.minimum(now + group, block_count - group)
+                for u in range(group):
+                    hidden = dot(w1[...], x_refs[phase][u][0:depth, :]).astype(jnp.bfloat16)
+                    hidden_refs[phase][u][0:hidden_rows, :] = jnp.maximum(hidden, jnp.zeros_like(hidden))
+                    build_taps(x_refs[1 - phase][u], after + u)
+                if target is not None:
+                    for u in range(group):
+                        add_block(now + u - group - 1, True)
+                if beside is not None and phase == 0:
+                    beside(i)
+                for u in range(group):
+                    y_s[now + u + LAG, 0:out_rows, :] = dot(w2[...], hidden_refs[phase][u][0:hidden_rows, :])
+
+        if target is not None:
+            for block in range(block_count - group - 1, block_count):
+                add_block(block, False)
+
+    def collapse(plane, slot):
+        def merged(s):
             at = s * 2 * BLOCK
-            merged = []
+            out = []
             for j in range(tiles):
                 cut = slice(j * LANES, (j + 1) * LANES)
-                outer = jnp.where(row == 0, y_s[slot - 1, at + BLOCK:at + 2 * BLOCK, cut], 0.0)
-                outer = jnp.where(row == BLOCK - 1, y_s[slot + 1, at + BLOCK:at + 2 * BLOCK, cut], outer)
-                merged.append(y_s[slot, at:at + BLOCK, cut] + outer)
-            moved = shift_tiles(merged, step)
-            total_value = moved if total_value is None else [a + b for a, b in zip(total_value, moved)]
-        return total_value
-
-    def update(field, shifts, shift_tiles, block_first, block_count):
-        @pl.loop(0, block_count)
-        def _(i):
-            base = pl.multiple_of(PAD + (block_first + i) * BLOCK, BLOCK)
-            for j, value in enumerate(collapse(shifts, shift_tiles, i + 1)):
-                field[j, pl.ds(base, BLOCK), :] += value
+                outer = jnp.where(masks["rows"][0], y_s[slot - 1, at + BLOCK:at + 2 * BLOCK, cut], 0.0)
+                outer = jnp.where(masks["rows"][BLOCK - 1], y_s[slot + 1, at + BLOCK:at + 2 * BLOCK, cut], outer)
+                out.append(y_s[slot, at:at + BLOCK, cut] + outer)
+            return out
+
+        return plane[2](merged, masks)
 
     def block_range(reach, own_count=row_count // BLOCK):
         count = min(blocks, own_count + 2 * reach)
@@ -256,26 +300,28 @@
 
     first, count = block_range(7)
     forward(jnp.int32(-BLOCK), total + 2 * BLOCK, 0, total)
-    network((h_s, a_s, sino_s), DUAL_SHIFTS, shift_dual, w1d, w2d, first, count)
-    update(h_s, DUAL_SHIFTS, shift_dual, first, count)
+    if count // 4 == cells // 256:
+        network((h_s, a_s, sino_s), DUAL, w1d, w2d, first, count, h_s, transpose_part)
+    else:
+        network((h_s, a_s, sino_s), DUAL, w1d, w2d, first, count, h_s)
+        for n in range(cells // 256):
+            transpose_part(n)
     first, count = block_range(5)
     adjoint(first * BLOCK, count * BLOCK)
-    network((f_s, b_s), PRIMAL_SHIFTS, shift_primal, w1p, w2p, first, count)
-    update(f_s, PRIMAL_SHIFTS, shift_primal, first, count)
+    network((f_s, b_s), PRIMAL, w1p, w2p, first, count, f_s)
 
     t_count = min(total + 2 * BLOCK, row_count + 10 * BLOCK)
     t_first = jnp.clip(own - 5 * BLOCK, -BLOCK, total + BLOCK - t_count)
     first, count = block_range(3)
     forward(t_first, t_count, first * BLOCK, count * BLOCK)
-    network((h_s, a_s, sino_s), DUAL_SHIFTS, shift_dual, w1d, w2d, first, count)
-    update(h_s, DUAL_SHIFTS, shift_dual, first, count)
+    network((h_s, a_s, sino_s), DUAL, w1d, w2d, first, count, h_s)
     first, count = block_range(1)
     adjoint(first * BLOCK, count * BLOCK)
-    network((f_s, b_s), PRIMAL_SHIFTS, shift_primal, w1p, w2p, first, count)
+    network((f_s, b_s), PRIMAL, w1p, w2p, first, count)
     for i in range(row_count // BLOCK):
-        slot = own_block - first + i + 1
+        slot = own_block - first + i + LAG
         base = pl.multiple_of(PAD + own + i * BLOCK, BLOCK)
-        for j, value in enumerate(collapse(PRIMAL_SHIFTS, shift_primal, slot)):
+        for j, value in enumerate(collapse(PRIMAL, slot)):
             out[i * BLOCK:(i + 1) * BLOCK, j * LANES:(j + 1) * LANES] = f_s[j, pl.ds(base, BLOCK), :] + value
 
 def gather(block, count):
@@ -327,8 +373,8 @@
         functools.partial(prepare, (dual_in.shape[::-1], primal_in.shape[::-1])),
         out_shape=[
             jax.ShapeDtypeStruct(shape, jnp.bfloat16) for shape in (
-                (BLOCK * dual_hidden, 128), (48, BLOCK * dual_hidden),
-                (BLOCK * primal_hidden, 256), (144, BLOCK * primal_hidden))
+                (BLOCK * dual_hidden, 96), (48, BLOCK * dual_hidden),
+                (BLOCK * primal_hidden, 224), (144, BLOCK * primal_hidden))
         ],
         in_specs=[whole],
         out_specs=[whole] * 4,
@@ -343,12 +389,11 @@
         in_specs=[pl.BlockSpec(memory_space=pltpu.SMEM)] + [whole] * len(operands),
         out_specs=whole,
         scratch_shapes=[field] * 6 + [
-            pltpu.VMEM((256, cells), jnp.bfloat16),
-            pltpu.VMEM((256, cells), jnp.bfloat16),
-            pltpu.VMEM((BLOCK * primal_hidden, cells), jnp.bfloat16),
-            pltpu.VMEM((BLOCK * primal_hidden, cells), jnp.bfloat16),
-            pltpu.VMEM((min(blocks, 16) + 2, 144, cells), jnp.float32),
+            *[pltpu.VMEM((224, cells), jnp.bfloat16)] * 4,
+            *[pltpu.VMEM((BLOCK * primal_hidden, cells), jnp.bfloat16)] * 4,
+            pltpu.VMEM((min(blocks, 16) + LAG + 1, 144, cells), jnp.float32),
             pltpu.VMEM((total + 2 * BLOCK, 3 * cells), jnp.bfloat16),
+            pltpu.VMEM((3 * cells, cells), jnp.bfloat16),
         ],
         compiler_params=pltpu.CompilerParams(vmem_limit_bytes=32 * 1024 * 1024),
         name="iterate",

time: 42.3 us -> 36 us (0.85)
  Pallas kernels: 29.9 us -> 23.6 us
    pallas_call x1, Pallas kernels: 29 us -> 22.7 us  [per_device(): pl.pallas_call(functools.partial(kernel, (window, tiles)), out_shape=jax....]
  transfers between devices with their start and end apart: 7 -> 7, of which waited for: 3 -> 3; matrix products, arithmetic and copies ran while one was open for 6% -> 8% of each run, Pallas kernels for 2% -> 3%
where the time goes in v3:
time: 36 us; the launch traced here: 35.6 us
  Pallas kernels  23.6 us (66%)
  starting transfers between devices  6.74 us (19%)
  local copies, waits for them, and re-layouts  2.63 us (7%)
  waiting for transfers between devices  1.63 us (5%)
  other arithmetic  0.99 us (3%)
    pallas_call x1, Pallas kernels, per_device(): pl.pallas_call(functools.partial(kernel, (window, tiles)), out_shape=jax....  22.7 us
    ppermute x7, starting transfers between devices, swap(): return lax.ppermute(x, 'gz', [(i, i ^ bits) for i in range(count)])  6.74 us
    ppermute x7, waiting for transfers between devices, swap(): return lax.ppermute(x, 'gz', [(i, i ^ bits) for i in range(count)])  1.63 us
    pallas_call x1, Pallas kernels, per_device(): pl.pallas_call(functools.partial(prepare, (dual_in.shape[::-1], primal_in...  0.92 us
    concatenate x1, other arithmetic, per_device(): jnp.concatenate([jnp.pad(p, ((0, -p.shape[0] % 16), (0, primal_hidden - p...  0.9 us
    another operation x1, local copies, waits for them, and re-layouts  0.89 us
    squeeze x1, local copies, waits for them, and re-layouts, per_device(): own_start = start_volume[segment]  0.84 us
    unnamed x5, local copies, waits for them, and re-layouts  0.79 us
  transfers between devices with their start and end apart: 7, of which 3 were waited for; matrix products, arithmetic and copies ran while one was open for 8% of the time, Pallas kernels for 3%

profile of v3, /device:TPU:1, one launch (start us, length us, event | category | flops | bytes accessed | tf_op | source)
XLA Modules:
  0.0 35.6 jit_solution(2994383989437530500)
XLA Ops:
  0.0 0.0 copy-start
  0.0 0.9 %dynamic-slice_convert_fusion = (bf16[1,16,1024]{2,1,0:T(8,128)(2,1)S(1)}, bf16[1,16,1024]{2,1,0:T(8,128)(2,1)S(1)}) fusion(f32[4,16,1024]{2,1,0:T(8,128)} %param.9, s32[]{:T(128)S(6)} %select_n.2, f32[4,16,1024]{2,1,0:T(8,128)} %param.8), kind=kLoop, calls=%fused_computation.13 | loop fusion | bytes 131076 | tf_op jit(solution)/shard_map/convert.1
  0.9 4.2 %collective-permute-start.5 = (bf16[2,16,1024]{2,1,0:T(8,128)(2,1)S(1)}, bf16[2,16,1024]{2,1,0:T(8,128)(2,1)S(1)}, u32[]{:S(2)}, u32[]{:S(2)}) collective-permute-start(bf16[2,16,1024]{2,1,0:T(8,128)(2,1)S(1)} %pad_maximum_fusion.refs_0_), channel_id=1, source_target_pairs={{0,6},{1,7},{2,4},{3,5},{4,2},{5,3},{6,0},{7,1},{8,14},{9,15},{10,... | collective-permute-start | bytes 196616 | tf_op jit(solution)/shard_map/ppermute | solution.py:332
  5.1 0.0 collective-permute-start.3
  5.1 0.4 %collective-permute-start.1 = (bf16[2,16,1024]{2,1,0:T(8,128)(2,1)S(1)}, bf16[2,16,1024]{2,1,0:T(8,128)(2,1)S(1)}, u32[]{:S(2)}, u32[]{:S(2)}) collective-permute-start(bf16[2,16,1024]{2,1,0:T(8,128)(2,1)S(1)} %pad_maximum_fusion.refs_0_), channel_id=1, source_target_pairs={{0,2},{1,3},{2,0},{3,1},{4,6},{5,7},{6,4},{7,5},{8,10},{9,11},{10,... | collective-permute-start | bytes 196616 | tf_op jit(solution)/shard_map/ppermute | solution.py:332
  5.5 1.2 %collective-permute-start = (bf16[2,16,1024]{2,1,0:T(8,128)(2,1)S(1)}, bf16[2,16,1024]{2,1,0:T(8,128)(2,1)S(1)}, u32[]{:S(2)}, u32[]{:S(2)}) collective-permute-start(bf16[2,16,1024]{2,1,0:T(8,128)(2,1)S(1)} %pad_maximum_fusion.refs_0_), channel_id=1, source_target_pairs={{0,1},{1,0},{2,3},{3,2},{4,5},{5,4},{6,7},{7,6},{8,9},{9,8},{10,11... | collective-permute-start | bytes 196616 | tf_op jit(solution)/shard_map/ppermute | solution.py:332
  6.7 0.8 %dynamic-slice_bitcast_fusion.own_start = f32[16,1024]{1,0:T(8,128)S(1)} fusion(f32[4,16,1024]{2,1,0:T(8,128)} %param.8, s32[]{:T(128)S(6)} %select_n.2), kind=kLoop, calls=%fused_computation.15 | loop fusion | bytes 131076 | tf_op jit(solution)/shard_map/squeeze | solution.py:354
  7.6 0.1 stack.40
  7.7 0.8 %copy.9 = bf16[32,27]{0,1:T(8,128)(2,1)S(1)} copy(bf16[32,27]{1,0:T(8,128)(2,1)} %param.12) | data formatting | bytes 3456 | tf_op args[4]
  8.5 0.9 %fusion.7.weights = bf16[144,64]{1,0:T(8,128)(2,1)S(1)} fusion(bf16[27,64]{1,0:T(8,128)(2,1)} %param.15, bf16[54,64]{1,0:T(8,128)(2,1)} %bitcast.18, bf16[9,32]{1,0:T(8,128)(2,1)} %param.13, bf16[27,32]{1,0:T(8,128)(2,1)S(1)} %bitcast.17), kind=kLoop, calls=%fused_computation.17 | loop fusion | flops 184320 | bytes 31104 | tf_op jit(solution)/shard_map/concatenate | solution.py:365
  9.4 0.9 %prepare.1 = (bf16[256,96]{1,0:T(8,128)(2,1)S(1)}, bf16[48,256]{1,0:T(8,128)(2,1)S(1)}, bf16[512,224]{1,0:T(8,128)(2,1)S(1)}, bf16[144,512]{1,0:T(8,128)(2,1)S(1)}) custom-call(bf16[144,64]{1,0:T(8,128)(2,1)S(1)} %fusion.7.weights), custom_call_target="tpu_custom_call" | custom-call | flops 2000000000 | bytes 8000000 | tf_op jit(solution)/shard_map/prepare/pallas_call | solution.py:372
  10.3 0.0 copy-done
  10.3 0.0 collective-permute-done.5.refs_6_
  10.3 0.1 collective-permute-start.6
  10.4 0.4 %collective-permute-done.3.refs_4_ = bf16[2,16,1024]{2,1,0:T(8,128)(2,1)S(1)} collective-permute-done((bf16[2,16,1024]{2,1,0:T(8,128)(2,1)S(1)}, bf16[2,16,1024]{2,1,0:T(8,128)(2,1)S(1)}, u32[]{:S(2)}, u32[]{:S(2)}) %collective-permute-start.3) | collective-permute-done | bytes 65568 | tf_op jit(solution)/shard_map/ppermute | solution.py:332
  10.8 0.8 %collective-permute-start.4 = (bf16[2,16,1024]{2,1,0:T(8,128)(2,1)S(1)}, bf16[2,16,1024]{2,1,0:T(8,128)(2,1)S(1)}, u32[]{:S(2)}, u32[]{:S(2)}) collective-permute-start(bf16[2,16,1024]{2,1,0:T(8,128)(2,1)S(1)} %collective-permute-done.3.refs_4_), channel_id=1, source_target_pairs={{0,1},{1,0},{2,3},{3,2},{4,5},{5,4},{6,7},{7,6},{8,9},{9,8},{10,11... | collective-permute-start | bytes 196616 | tf_op jit(solution)/shard_map/ppermute | solution.py:332
  11.7 0.0 collective-permute-done.1.refs_2_
  11.7 0.0 collective-permute-start.2
  11.7 0.1 pad_add_fusion.info
  11.8 0.0 collective-permute-done.refs_1_
  11.8 0.0 collective-permute-done.6.refs_7_
  11.8 0.8 %collective-permute-done.4.refs_5_ = bf16[2,16,1024]{2,1,0:T(8,128)(2,1)S(1)} collective-permute-done((bf16[2,16,1024]{2,1,0:T(8,128)(2,1)S(1)}, bf16[2,16,1024]{2,1,0:T(8,128)(2,1)S(1)}, u32[]{:S(2)}, u32[]{:S(2)}) %collective-permute-start.4) | collective-permute-done | bytes 65568 | tf_op jit(solution)/shard_map/ppermute | solution.py:332
  12.6 0.4 collective-permute-done.2.refs_3_
  13.0 22.7 %iterate.1 = f32[16,1024]{1,0:T(8,128)} custom-call(s32[17]{0:T(128)S(1)} %pad_add_fusion.info, f32[16,1024]{1,0:T(8,128)S(1)} %dynamic-slice_bitcast_fusion.own_start, bf16[2,16,1024]{2,1,0:T(8,128)(2,1)S(1)} %pad_maximum_fusion.refs_0_, bf16[2,16,1024]{2,1,0:T(8,128)(2,1)S(1)} %collective-permute-done.refs_1_, ...), custom_call_target="tpu_custom_call" | custom-call | tf_op jit(solution)/shard_map/iterate/pallas_call | solution.py:386
  (5 shorter events, 0.0 us)
Async XLA Ops:
  0.0 10.3 %copy-start = (s32[4,8]{1,0:T(4,128)S(1)}, s32[4,8]{1,0:T(4,128)}, u32[]{:S(2)}) copy-start(s32[4,8]{1,0:T(4,128)} %param.10) | copy-start | bytes 388
  0.9 9.4 %collective-permute-start.5 = (bf16[2,16,1024]{2,1,0:T(8,128)(2,1)S(1)}, bf16[2,16,1024]{2,1,0:T(8,128)(2,1)S(1)}, u32[]{:S(2)}, u32[]{:S(2)}) collective-permute-start(bf16[2,16,1024]{2,1,0:T(8,128)(2,1)S(1)} %pad_maximum_fusion.refs_0_), channel_id=1, source_target_pairs={{0,6},{1,7},{2,4},{3,5},{4,2},{5,3},{6,0},{7,1},{8,14},{9,15},{10,... | collective-permute-start | bytes 196616 | tf_op jit(solution)/shard_map/ppermute | solution.py:332
  5.1 5.7 %collective-permute-start.3 = (bf16[2,16,1024]{2,1,0:T(8,128)(2,1)S(1)}, bf16[2,16,1024]{2,1,0:T(8,128)(2,1)S(1)}, u32[]{:S(2)}, u32[]{:S(2)}) collective-permute-start(bf16[2,16,1024]{2,1,0:T(8,128)(2,1)S(1)} %pad_maximum_fusion.refs_0_), channel_id=1, source_target_pairs={{0,4},{1,5},{2,6},{3,7},{4,0},{5,1},{6,2},{7,3},{8,12},{9,13},{10,... | collective-permute-start | bytes 196616 | tf_op jit(solution)/shard_map/ppermute | solution.py:332
  5.1 6.6 %collective-permute-start.1 = (bf16[2,16,1024]{2,1,0:T(8,128)(2,1)S(1)}, bf16[2,16,1024]{2,1,0:T(8,128)(2,1)S(1)}, u32[]{:S(2)}, u32[]{:S(2)}) collective-permute-start(bf16[2,16,1024]{2,1,0:T(8,128)(2,1)S(1)} %pad_maximum_fusion.refs_0_), channel_id=1, source_target_pairs={{0,2},{1,3},{2,0},{3,1},{4,6},{5,7},{6,4},{7,5},{8,10},{9,11},{10,... | collective-permute-start | bytes 196616 | tf_op jit(solution)/shard_map/ppermute | solution.py:332
  5.5 6.3 %collective-permute-start = (bf16[2,16,1024]{2,1,0:T(8,128)(2,1)S(1)}, bf16[2,16,1024]{2,1,0:T(8,128)(2,1)S(1)}, u32[]{:S(2)}, u32[]{:S(2)}) collective-permute-start(bf16[2,16,1024]{2,1,0:T(8,128)(2,1)S(1)} %pad_maximum_fusion.refs_0_), channel_id=1, source_target_pairs={{0,1},{1,0},{2,3},{3,2},{4,5},{5,4},{6,7},{7,6},{8,9},{9,8},{10,11... | collective-permute-start | bytes 196616 | tf_op jit(solution)/shard_map/ppermute | solution.py:332
  8.5 4.5 %copy-start.1 = (bf16[3,1024,1024]{2,1,0:T(8,128)(2,1)S(1)}, bf16[3,1024,1024]{2,1,0:T(8,128)(2,1)}, u32[]{:S(2)}) copy-start(bf16[3,1024,1024]{2,1,0:T(8,128)(2,1)} %param.11) | copy-start | bytes 18874372
  10.3 1.5 %collective-permute-start.6 = (bf16[2,16,1024]{2,1,0:T(8,128)(2,1)S(1)}, bf16[2,16,1024]{2,1,0:T(8,128)(2,1)S(1)}, u32[]{:S(2)}, u32[]{:S(2)}) collective-permute-start(bf16[2,16,1024]{2,1,0:T(8,128)(2,1)S(1)} %collective-permute-done.5.refs_6_), channel_id=1, source_target_pairs={{0,1},{1,0},{2,3},{3,2},{4,5},{5,4},{6,7},{7,6},{8,9},{9,8},{10,11... | collective-permute-start | bytes 196616 | tf_op jit(solution)/shard_map/ppermute | solution.py:332
  10.8 1.7 %collective-permute-start.4 = (bf16[2,16,1024]{2,1,0:T(8,128)(2,1)S(1)}, bf16[2,16,1024]{2,1,0:T(8,128)(2,1)S(1)}, u32[]{:S(2)}, u32[]{:S(2)}) collective-permute-start(bf16[2,16,1024]{2,1,0:T(8,128)(2,1)S(1)} %collective-permute-done.3.refs_4_), channel_id=1, source_target_pairs={{0,1},{1,0},{2,3},{3,2},{4,5},{5,4},{6,7},{7,6},{8,9},{9,8},{10,11... | collective-permute-start | bytes 196616 | tf_op jit(solution)/shard_map/ppermute | solution.py:332
  11.7 1.3 %collective-permute-start.2 = (bf16[2,16,1024]{2,1,0:T(8,128)(2,1)S(1)}, bf16[2,16,1024]{2,1,0:T(8,128)(2,1)S(1)}, u32[]{:S(2)}, u32[]{:S(2)}) collective-permute-start(bf16[2,16,1024]{2,1,0:T(8,128)(2,1)S(1)} %collective-permute-done.1.refs_2_), channel_id=1, source_target_pairs={{0,1},{1,0},{2,3},{3,2},{4,5},{5,4},{6,7},{7,6},{8,9},{9,8},{10,11... | collective-permute-start | bytes 196616 | tf_op jit(solution)/shard_map/ppermute | solution.py:332

commit v4 on v3

--- a/solution.py
+++ b/solution.py
@@ -14,6 +14,8 @@
 PAD = 16
 HALO_BLOCKS = 5
 LAG = 4
+STEPS = 2
+UNROLLED = 12
 
 
 def dot(a, b):
@@ -162,10 +164,8 @@
     x_refs, hidden_refs = ((x_0, x_1), (x_2, x_3)), ((hidden_0, hidden_1), (hidden_2, hidden_3))
     row_count = own_start.shape[0]
     total = window * row_count
-    blocks = total // BLOCK
     cells = tiles * LANES
     own = info[0]
-    own_block = own // BLOCK
 
     masks = masks_of()
 
@@ -220,18 +220,17 @@
                 b_s[2 * n + part, pl.ds(pl.multiple_of(PAD + z_first, BLOCK), count), :] = value[
                     :, part * LANES:(part + 1) * LANES]
 
-    def network(fields, plane, w1, w2, block_first, block_count, target=None, beside=None):
+    def network(fields, plane, w1, w2, first_row, block_count, target, beside=None):
         count, shifted, _ = plane
         hidden_rows, depth = w1.shape
         out_rows = 2 * BLOCK * count
         group = len(x_refs[0])
-        groups = block_count // group
         edge = jnp.zeros((out_rows, cells), jnp.float32)
         for slot in (LAG - 1, block_count + LAG):
             y_s[slot, 0:out_rows, :] = edge
 
         def build_taps(x, block):
-            base = pl.multiple_of(PAD + (block_first + block) * BLOCK, BLOCK)
+            base = PAD + first_row + block * BLOCK
             mains = [[field[j, pl.ds(base, BLOCK), :] for j in range(tiles)] for field in fields]
             edges = []
             for j in range(tiles):
@@ -249,37 +248,51 @@
                     x[pair * 16:(pair + 1) * 16, j * LANES:(j + 1) * LANES] = jnp.concatenate(
                         [arrays[2 * pair][j], arrays[2 * pair + 1][j]], axis=0).astype(jnp.bfloat16)
 
-        def add_block(block, guarded):
+        def add_block(block):
             value = collapse(plane, block + LAG)
-            at = jnp.maximum(block, 0) if guarded else block
-            base = pl.multiple_of(PAD + (block_first + at) * BLOCK, BLOCK)
+            inside = isinstance(block, int)
+            base = PAD + first_row + (block if inside else jnp.maximum(block, 0)) * BLOCK
             for j in range(tiles):
-                part = jnp.where(block >= 0, value[j], 0.0) if guarded else value[j]
+                part = value[j] if inside else jnp.where(block >= 0, value[j], 0.0)
                 target[j, pl.ds(base, BLOCK), :] += part
+
+        def step(side, now, after, done):
+            for u in range(max(len(now), len(after))):
+                if u < len(now):
+                    hidden = dot(w1[...], x_refs[side][u][0:depth, :]).astype(jnp.bfloat16)
+                    hidden_refs[side][u][0:hidden_rows, :] = jnp.maximum(hidden, jnp.zeros_like(hidden))
+                if u < len(after):
+                    build_taps(x_refs[1 - side][u], after[u])
+            for block in done:
+                add_block(block)
+            for u, block in enumerate(now):
+                y_s[block + LAG, 0:out_rows, :] = dot(w2[...], hidden_refs[side][u][0:hidden_rows, :])
+
+        def blocks_from(start):
+            return [b for b in range(start, start + group) if 0 <= b < block_count]
 
         for u in range(group):
             build_taps(x_refs[0][u], u)
-
-        @pl.loop(0, groups // 2)
-        def _(i):
-            for phase in range(2):
-                now = (2 * i + phase) * group
-                after = jnp.minimum(now + group, block_count - group)
-                for u in range(group):
-                    hidden = dot(w1[...], x_refs[phase][u][0:depth, :]).astype(jnp.bfloat16)
-                    hidden_refs[phase][u][0:hidden_rows, :] = jnp.maximum(hidden, jnp.zeros_like(hidden))
-                    build_taps(x_refs[1 - phase][u], after + u)
-                if target is not None:
-                    for u in range(group):
-                        add_block(now + u - group - 1, True)
-                if beside is not None and phase == 0:
-                    beside(i)
-                for u in range(group):
-                    y_s[now + u + LAG, 0:out_rows, :] = dot(w2[...], hidden_refs[phase][u][0:hidden_rows, :])
-
-        if target is not None:
-            for block in range(block_count - group - 1, block_count):
-                add_block(block, False)
+        per_turn = STEPS * group
+        if block_count % per_turn == 0 and block_count > UNROLLED:
+            @pl.loop(0, block_count // per_turn)
+            def _(i):
+                for phase in range(STEPS):
+                    now = i * per_turn + phase * group
+                    after = jnp.minimum(now + group, block_count - group)
+                    step(phase % 2, [now + u for u in range(group)], [after + u for u in range(group)],
+                         [now + u - group - 1 for u in range(group)])
+                    if beside is not None and phase % 2 == 0:
+                        beside(i * (STEPS // 2) + phase // 2)
+        else:
+            for turn in range(-(-block_count // group)):
+                now = turn * group
+                step(turn % 2, blocks_from(now), blocks_from(now + group), blocks_from(now - group - 1))
+                if beside is not None and turn % 2 == 0:
+                    beside(turn // 2)
+        last = -(-block_count // group) * group
+        for block in range(max(last - group - 1, 0), block_count):
+            add_block(block)
 
     def collapse(plane, slot):
         def merged(s):
@@ -294,35 +307,36 @@
 
         return plane[2](merged, masks)
 
-    def block_range(reach, own_count=row_count // BLOCK):
-        count = min(blocks, own_count + 2 * reach)
-        return jnp.clip(own_block - reach, 0, blocks - count), count
-
-    first, count = block_range(7)
+    def reached(reach, unit=BLOCK):
+        count = min(-(-(row_count + 2 * reach) // unit) * unit, total)
+        return jnp.clip(own - (count - row_count) // 2, 0, total - count), count
+
+    first, count = reached(3 * row_count + 7)
     forward(jnp.int32(-BLOCK), total + 2 * BLOCK, 0, total)
-    if count // 4 == cells // 256:
-        network((h_s, a_s, sino_s), DUAL, w1d, w2d, first, count, h_s, transpose_part)
+    quarters = cells // 256
+    if count // (4 * BLOCK) == quarters:
+        network((h_s, a_s, sino_s), DUAL, w1d, w2d, first, count // BLOCK, h_s, transpose_part)
     else:
-        network((h_s, a_s, sino_s), DUAL, w1d, w2d, first, count, h_s)
-        for n in range(cells // 256):
+        network((h_s, a_s, sino_s), DUAL, w1d, w2d, first, count // BLOCK, h_s)
+        for n in range(quarters):
             transpose_part(n)
-    first, count = block_range(5)
-    adjoint(first * BLOCK, count * BLOCK)
-    network((f_s, b_s), PRIMAL, w1p, w2p, first, count, f_s)
+    first, count = reached(2 * row_count + 5, 2 * BLOCK)
+    adjoint(first, count)
+    network((f_s, b_s), PRIMAL, w1p, w2p, first, count // BLOCK, f_s)
 
     t_count = min(total + 2 * BLOCK, row_count + 10 * BLOCK)
     t_first = jnp.clip(own - 5 * BLOCK, -BLOCK, total + BLOCK - t_count)
-    first, count = block_range(3)
-    forward(t_first, t_count, first * BLOCK, count * BLOCK)
-    network((h_s, a_s, sino_s), DUAL, w1d, w2d, first, count, h_s)
-    first, count = block_range(1)
-    adjoint(first * BLOCK, count * BLOCK)
-    network((f_s, b_s), PRIMAL, w1p, w2p, first, count)
-    for i in range(row_count // BLOCK):
-        slot = own_block - first + i + LAG
-        base = pl.multiple_of(PAD + own + i * BLOCK, BLOCK)
-        for j, value in enumerate(collapse(PRIMAL, slot)):
-            out[i * BLOCK:(i + 1) * BLOCK, j * LANES:(j + 1) * LANES] = f_s[j, pl.ds(base, BLOCK), :] + value
+    first, count = reached(row_count + 4, 2 * BLOCK)
+    forward(t_first, t_count, first, count)
+    first, count = reached(row_count + 3)
+    network((h_s, a_s, sino_s), DUAL, w1d, w2d, first, count // BLOCK, h_s)
+    first, count = reached(2, 2 * BLOCK)
+    adjoint(first, count)
+    first, count = reached(1)
+    network((f_s, b_s), PRIMAL, w1p, w2p, first, count // BLOCK, f_s)
+    for j in range(tiles):
+        out[:, j * LANES:(j + 1) * LANES] = f_s[j, pl.ds(pl.multiple_of(own + PAD, BLOCK), row_count), :]
+
 
 def gather(block, count):
     me = lax.axis_index("gz")
@@ -332,9 +346,7 @@
             return lax.ppermute(x, "gz", [(i, i ^ bits) for i in range(count)])
 
         held = {0: block}
-        for bits in range(2, count, 4):
-            held[bits] = swap(block, bits)
-        for bits in range(4, count, 4):
+        for bits in [2] * (count > 2) + list(range(count - 2, 3, -2)):
             held[bits] = swap(block, bits)
         if count > 1:
             for bits in list(held):

time: 36 us -> 34.3 us (0.953)
  Pallas kernels: 23.6 us -> 22 us
    pallas_call x1, Pallas kernels: 22.7 us -> 21 us  [per_device(): pl.pallas_call(functools.partial(kernel, (window, tiles)), out_shape=jax....]
where the time goes in v4:
time: 34.3 us; the launch traced here: 34 us
  Pallas kernels  22 us (64%)
  starting transfers between devices  6.74 us (20%)
  local copies, waits for them, and re-layouts  2.63 us (8%)
  waiting for transfers between devices  1.63 us (5%)
  other arithmetic  0.99 us (3%)
    pallas_call x1, Pallas kernels, per_device(): pl.pallas_call(functools.partial(kernel, (window, tiles)), out_shape=jax....  21 us
    ppermute x7, starting transfers between devices, swap(): return lax.ppermute(x, 'gz', [(i, i ^ bits) for i in range(count)])  6.74 us
    ppermute x7, waiting for transfers between devices, swap(): return lax.ppermute(x, 'gz', [(i, i ^ bits) for i in range(count)])  1.63 us
    pallas_call x1, Pallas kernels, per_device(): pl.pallas_call(functools.partial(prepare, (dual_in.shape[::-1], primal_in...  0.92 us
    concatenate x1, other arithmetic, per_device(): jnp.concatenate([jnp.pad(p, ((0, -p.shape[0] % 16), (0, primal_hidden - p...  0.9 us
    another operation x1, local copies, waits for them, and re-layouts  0.89 us
    squeeze x1, local copies, waits for them, and re-layouts, per_device(): own_start = start_volume[segment]  0.84 us
    unnamed x5, local copies, waits for them, and re-layouts  0.79 us
  transfers between devices with their start and end apart: 7, of which 3 were waited for; matrix products, arithmetic and copies ran while one was open for 8% of the time, Pallas kernels for 3%

profile of v4, /device:TPU:1, one launch (start us, length us, event | category | flops | bytes accessed | tf_op | source)
XLA Modules:
  0.0 34.0 jit_solution(5679271879793712565)
XLA Ops:
  0.0 0.0 copy-start
  0.0 0.9 %dynamic-slice_convert_fusion = (bf16[1,16,1024]{2,1,0:T(8,128)(2,1)S(1)}, bf16[1,16,1024]{2,1,0:T(8,128)(2,1)S(1)}) fusion(f32[4,16,1024]{2,1,0:T(8,128)} %param.9, s32[]{:T(128)S(6)} %select_n.2, f32[4,16,1024]{2,1,0:T(8,128)} %param.8), kind=kLoop, calls=%fused_computation.13 | loop fusion | bytes 131076 | tf_op jit(solution)/shard_map/convert.1
  0.9 4.2 %collective-permute-start.5 = (bf16[2,16,1024]{2,1,0:T(8,128)(2,1)S(1)}, bf16[2,16,1024]{2,1,0:T(8,128)(2,1)S(1)}, u32[]{:S(2)}, u32[]{:S(2)}) collective-permute-start(bf16[2,16,1024]{2,1,0:T(8,128)(2,1)S(1)} %pad_maximum_fusion.refs_0_), channel_id=1, source_target_pairs={{0,6},{1,7},{2,4},{3,5},{4,2},{5,3},{6,0},{7,1},{8,14},{9,15},{10,... | collective-permute-start | bytes 196616 | tf_op jit(solution)/shard_map/ppermute | solution.py:346
  5.1 0.0 collective-permute-start.3
  5.1 0.4 %collective-permute-start.1 = (bf16[2,16,1024]{2,1,0:T(8,128)(2,1)S(1)}, bf16[2,16,1024]{2,1,0:T(8,128)(2,1)S(1)}, u32[]{:S(2)}, u32[]{:S(2)}) collective-permute-start(bf16[2,16,1024]{2,1,0:T(8,128)(2,1)S(1)} %pad_maximum_fusion.refs_0_), channel_id=1, source_target_pairs={{0,2},{1,3},{2,0},{3,1},{4,6},{5,7},{6,4},{7,5},{8,10},{9,11},{10,... | collective-permute-start | bytes 196616 | tf_op jit(solution)/shard_map/ppermute | solution.py:346
  5.5 1.2 %collective-permute-start = (bf16[2,16,1024]{2,1,0:T(8,128)(2,1)S(1)}, bf16[2,16,1024]{2,1,0:T(8,128)(2,1)S(1)}, u32[]{:S(2)}, u32[]{:S(2)}) collective-permute-start(bf16[2,16,1024]{2,1,0:T(8,128)(2,1)S(1)} %pad_maximum_fusion.refs_0_), channel_id=1, source_target_pairs={{0,1},{1,0},{2,3},{3,2},{4,5},{5,4},{6,7},{7,6},{8,9},{9,8},{10,11... | collective-permute-start | bytes 196616 | tf_op jit(solution)/shard_map/ppermute | solution.py:346
  6.7 0.8 %dynamic-slice_bitcast_fusion.own_start = f32[16,1024]{1,0:T(8,128)S(1)} fusion(f32[4,16,1024]{2,1,0:T(8,128)} %param.8, s32[]{:T(128)S(6)} %select_n.2), kind=kLoop, calls=%fused_computation.15 | loop fusion | bytes 131076 | tf_op jit(solution)/shard_map/squeeze | solution.py:366
  7.6 0.1 stack.40
  7.7 0.8 %copy.9 = bf16[32,27]{0,1:T(8,128)(2,1)S(1)} copy(bf16[32,27]{1,0:T(8,128)(2,1)} %param.12) | data formatting | bytes 3456 | tf_op args[4]
  8.5 0.9 %fusion.7.weights = bf16[144,64]{1,0:T(8,128)(2,1)S(1)} fusion(bf16[27,64]{1,0:T(8,128)(2,1)} %param.15, bf16[54,64]{1,0:T(8,128)(2,1)} %bitcast.18, bf16[9,32]{1,0:T(8,128)(2,1)} %param.13, bf16[27,32]{1,0:T(8,128)(2,1)S(1)} %bitcast.17), kind=kLoop, calls=%fused_computation.17 | loop fusion | flops 184320 | bytes 31104 | tf_op jit(solution)/shard_map/concatenate | solution.py:377
  9.4 0.9 %prepare.1 = (bf16[256,96]{1,0:T(8,128)(2,1)S(1)}, bf16[48,256]{1,0:T(8,128)(2,1)S(1)}, bf16[512,224]{1,0:T(8,128)(2,1)S(1)}, bf16[144,512]{1,0:T(8,128)(2,1)S(1)}) custom-call(bf16[144,64]{1,0:T(8,128)(2,1)S(1)} %fusion.7.weights), custom_call_target="tpu_custom_call" | custom-call | flops 2000000000 | bytes 8000000 | tf_op jit(solution)/shard_map/prepare/pallas_call | solution.py:384
  10.3 0.0 copy-done
  10.3 0.0 collective-permute-done.5.refs_6_
  10.3 0.1 collective-permute-start.6
  10.4 0.4 %collective-permute-done.3.refs_4_ = bf16[2,16,1024]{2,1,0:T(8,128)(2,1)S(1)} collective-permute-done((bf16[2,16,1024]{2,1,0:T(8,128)(2,1)S(1)}, bf16[2,16,1024]{2,1,0:T(8,128)(2,1)S(1)}, u32[]{:S(2)}, u32[]{:S(2)}) %collective-permute-start.3) | collective-permute-done | bytes 65568 | tf_op jit(solution)/shard_map/ppermute | solution.py:346
  10.8 0.8 %collective-permute-start.4 = (bf16[2,16,1024]{2,1,0:T(8,128)(2,1)S(1)}, bf16[2,16,1024]{2,1,0:T(8,128)(2,1)S(1)}, u32[]{:S(2)}, u32[]{:S(2)}) collective-permute-start(bf16[2,16,1024]{2,1,0:T(8,128)(2,1)S(1)} %collective-permute-done.3.refs_4_), channel_id=1, source_target_pairs={{0,1},{1,0},{2,3},{3,2},{4,5},{5,4},{6,7},{7,6},{8,9},{9,8},{10,11... | collective-permute-start | bytes 196616 | tf_op jit(solution)/shard_map/ppermute | solution.py:346
  11.7 0.0 collective-permute-done.1.refs_2_
  11.7 0.0 collective-permute-start.2
  11.7 0.1 pad_add_fusion.info
  11.8 0.0 collective-permute-done.refs_1_
  11.8 0.0 collective-permute-done.6.refs_7_
  11.8 0.8 %collective-permute-done.4.refs_5_ = bf16[2,16,1024]{2,1,0:T(8,128)(2,1)S(1)} collective-permute-done((bf16[2,16,1024]{2,1,0:T(8,128)(2,1)S(1)}, bf16[2,16,1024]{2,1,0:T(8,128)(2,1)S(1)}, u32[]{:S(2)}, u32[]{:S(2)}) %collective-permute-start.4) | collective-permute-done | bytes 65568 | tf_op jit(solution)/shard_map/ppermute | solution.py:346
  12.6 0.4 %collective-permute-done.2.refs_3_ = bf16[2,16,1024]{2,1,0:T(8,128)(2,1)S(1)} collective-permute-done((bf16[2,16,1024]{2,1,0:T(8,128)(2,1)S(1)}, bf16[2,16,1024]{2,1,0:T(8,128)(2,1)S(1)}, u32[]{:S(2)}, u32[]{:S(2)}) %collective-permute-start.2) | collective-permute-done | bytes 65568 | tf_op jit(solution)/shard_map/ppermute | solution.py:346
  13.0 21.0 %iterate.1 = f32[16,1024]{1,0:T(8,128)} custom-call(s32[17]{0:T(128)S(1)} %pad_add_fusion.info, f32[16,1024]{1,0:T(8,128)S(1)} %dynamic-slice_bitcast_fusion.own_start, bf16[2,16,1024]{2,1,0:T(8,128)(2,1)S(1)} %pad_maximum_fusion.refs_0_, bf16[2,16,1024]{2,1,0:T(8,128)(2,1)S(1)} %collective-permute-done.refs_1_, ...), custom_call_target="tpu_custom_call" | custom-call | tf_op jit(solution)/shard_map/iterate/pallas_call | solution.py:398
  (5 shorter events, 0.0 us)
Async XLA Ops:
  0.0 10.3 %copy-start = (s32[4,8]{1,0:T(4,128)S(1)}, s32[4,8]{1,0:T(4,128)}, u32[]{:S(2)}) copy-start(s32[4,8]{1,0:T(4,128)} %param.10) | copy-start | bytes 388
  0.9 9.4 %collective-permute-start.5 = (bf16[2,16,1024]{2,1,0:T(8,128)(2,1)S(1)}, bf16[2,16,1024]{2,1,0:T(8,128)(2,1)S(1)}, u32[]{:S(2)}, u32[]{:S(2)}) collective-permute-start(bf16[2,16,1024]{2,1,0:T(8,128)(2,1)S(1)} %pad_maximum_fusion.refs_0_), channel_id=1, source_target_pairs={{0,6},{1,7},{2,4},{3,5},{4,2},{5,3},{6,0},{7,1},{8,14},{9,15},{10,... | collective-permute-start | bytes 196616 | tf_op jit(solution)/shard_map/ppermute | solution.py:346
  5.1 5.7 %collective-permute-start.3 = (bf16[2,16,1024]{2,1,0:T(8,128)(2,1)S(1)}, bf16[2,16,1024]{2,1,0:T(8,128)(2,1)S(1)}, u32[]{:S(2)}, u32[]{:S(2)}) collective-permute-start(bf16[2,16,1024]{2,1,0:T(8,128)(2,1)S(1)} %pad_maximum_fusion.refs_0_), channel_id=1, source_target_pairs={{0,4},{1,5},{2,6},{3,7},{4,0},{5,1},{6,2},{7,3},{8,12},{9,13},{10,... | collective-permute-start | bytes 196616 | tf_op jit(solution)/shard_map/ppermute | solution.py:346
  5.1 6.6 %collective-permute-start.1 = (bf16[2,16,1024]{2,1,0:T(8,128)(2,1)S(1)}, bf16[2,16,1024]{2,1,0:T(8,128)(2,1)S(1)}, u32[]{:S(2)}, u32[]{:S(2)}) collective-permute-start(bf16[2,16,1024]{2,1,0:T(8,128)(2,1)S(1)} %pad_maximum_fusion.refs_0_), channel_id=1, source_target_pairs={{0,2},{1,3},{2,0},{3,1},{4,6},{5,7},{6,4},{7,5},{8,10},{9,11},{10,... | collective-permute-start | bytes 196616 | tf_op jit(solution)/shard_map/ppermute | solution.py:346
  5.5 6.3 %collective-permute-start = (bf16[2,16,1024]{2,1,0:T(8,128)(2,1)S(1)}, bf16[2,16,1024]{2,1,0:T(8,128)(2,1)S(1)}, u32[]{:S(2)}, u32[]{:S(2)}) collective-permute-start(bf16[2,16,1024]{2,1,0:T(8,128)(2,1)S(1)} %pad_maximum_fusion.refs_0_), channel_id=1, source_target_pairs={{0,1},{1,0},{2,3},{3,2},{4,5},{5,4},{6,7},{7,6},{8,9},{9,8},{10,11... | collective-permute-start | bytes 196616 | tf_op jit(solution)/shard_map/ppermute | solution.py:346
  8.5 4.5 %copy-start.1 = (bf16[3,1024,1024]{2,1,0:T(8,128)(2,1)S(1)}, bf16[3,1024,1024]{2,1,0:T(8,128)(2,1)}, u32[]{:S(2)}) copy-start(bf16[3,1024,1024]{2,1,0:T(8,128)(2,1)} %param.11) | copy-start | bytes 18874372
  10.3 1.5 %collective-permute-start.6 = (bf16[2,16,1024]{2,1,0:T(8,128)(2,1)S(1)}, bf16[2,16,1024]{2,1,0:T(8,128)(2,1)S(1)}, u32[]{:S(2)}, u32[]{:S(2)}) collective-permute-start(bf16[2,16,1024]{2,1,0:T(8,128)(2,1)S(1)} %collective-permute-done.5.refs_6_), channel_id=1, source_target_pairs={{0,1},{1,0},{2,3},{3,2},{4,5},{5,4},{6,7},{7,6},{8,9},{9,8},{10,11... | collective-permute-start | bytes 196616 | tf_op jit(solution)/shard_map/ppermute | solution.py:346
  10.8 1.7 %collective-permute-start.4 = (bf16[2,16,1024]{2,1,0:T(8,128)(2,1)S(1)}, bf16[2,16,1024]{2,1,0:T(8,128)(2,1)S(1)}, u32[]{:S(2)}, u32[]{:S(2)}) collective-permute-start(bf16[2,16,1024]{2,1,0:T(8,128)(2,1)S(1)} %collective-permute-done.3.refs_4_), channel_id=1, source_target_pairs={{0,1},{1,0},{2,3},{3,2},{4,5},{5,4},{6,7},{7,6},{8,9},{9,8},{10,11... | collective-permute-start | bytes 196616 | tf_op jit(solution)/shard_map/ppermute | solution.py:346
  11.7 1.3 %collective-permute-start.2 = (bf16[2,16,1024]{2,1,0:T(8,128)(2,1)S(1)}, bf16[2,16,1024]{2,1,0:T(8,128)(2,1)S(1)}, u32[]{:S(2)}, u32[]{:S(2)}) collective-permute-start(bf16[2,16,1024]{2,1,0:T(8,128)(2,1)S(1)} %collective-permute-done.1.refs_2_), channel_id=1, source_target_pairs={{0,1},{1,0},{2,3},{3,2},{4,5},{5,4},{6,7},{7,6},{8,9},{9,8},{10,11... | collective-permute-start | bytes 196616 | tf_op jit(solution)/shard_map/ppermute | solution.py:346

commit v5 on v4

--- a/solution.py
+++ b/solution.py
@@ -155,14 +155,16 @@
     second_weights(parts[3], p_hidden, 9, w2p)
 
 
-def kernel(sizes, info, own_start, *refs):
+def kernel(sizes, info, volumes, *refs):
     window, tiles = sizes
     pieces = refs[:window]
     (projector, w1d, w2d, w1p, w2p, out, f_s, sino_s, t_s, a_s, h_s, b_s,
      x_0, x_1, x_2, x_3, hidden_0, hidden_1, hidden_2, hidden_3, y_s, lhs_s,
-     across_s) = refs[window:]
+     across_s, own_start, arrived) = refs[window:]
     x_refs, hidden_refs = ((x_0, x_1), (x_2, x_3)), ((hidden_0, hidden_1), (hidden_2, hidden_3))
     row_count = own_start.shape[0]
+    own_copy = pltpu.make_async_copy(volumes.at[info[1 + window + tiles]], own_start, arrived)
+    own_copy.start()
     total = window * row_count
     cells = tiles * LANES
     own = info[0]
@@ -184,6 +186,7 @@
             cut = slice(j * LANES, (j + 1) * LANES)
             f_s[j, pl.ds(at, row_count), :] = piece[0, :, cut].astype(jnp.float32)
             sino_s[j, pl.ds(at, row_count), :] = piece[1, :, cut].astype(jnp.float32)
+    own_copy.wait()
     for j in range(tiles):
         f_s[j, pl.ds(pl.multiple_of(own + PAD, BLOCK), row_count), :] = own_start[:, j * LANES:(j + 1) * LANES]
 
@@ -371,6 +374,7 @@
     info = jnp.concatenate([
         jnp.stack([jnp.int32(own)] + [jnp.int32(p) for p in places]) * row_count,
         offsets[segment],
+        segment.astype(jnp.int32)[None],
     ])
     dual_hidden, primal_hidden = dual_in.shape[0], primal_in.shape[0]
     parts = [dual_in.T, dual_out, primal_in.T, primal_out]
@@ -394,11 +398,12 @@
         compiler_params=pltpu.CompilerParams(vmem_limit_bytes=16 * 1024 * 1024),
         name="prepare",
     )(packed)
-    operands = [own_start, *pieces, flat, *weights]
+    operands = [start_volume, *pieces, flat, *weights]
     result = pl.pallas_call(
         functools.partial(kernel, (window, tiles)),
         out_shape=jax.ShapeDtypeStruct((row_count, cells), jnp.float32),
-        in_specs=[pl.BlockSpec(memory_space=pltpu.SMEM)] + [whole] * len(operands),
+        in_specs=[pl.BlockSpec(memory_space=pltpu.SMEM), pl.BlockSpec(memory_space=pl.ANY)]
+        + [whole] * (len(operands) - 1),
         out_specs=whole,
         scratch_shapes=[field] * 6 + [
             *[pltpu.VMEM((224, cells), jnp.bfloat16)] * 4,
@@ -406,6 +411,8 @@
             pltpu.VMEM((min(blocks, 16) + LAG + 1, 144, cells), jnp.float32),
             pltpu.VMEM((total + 2 * BLOCK, 3 * cells), jnp.bfloat16),
             pltpu.VMEM((3 * cells, cells), jnp.bfloat16),
+            pltpu.VMEM((row_count, cells), jnp.float32),
+            pltpu.SemaphoreType.DMA,
         ],
         compiler_params=pltpu.CompilerParams(vmem_limit_bytes=32 * 1024 * 1024),
         name="iterate",

time: 34.3 us -> 34.6 us (level)
  waiting for transfers between devices: 1.63 us -> 2.47 us
  local copies, waits for them, and re-layouts: 2.63 us -> 1.82 us
    squeeze x1 -> x0, local copies, waits for them, and re-layouts: 0.84 us -> none  [per_device(): own_start = start_volume[segment]]
    ppermute x7, waiting for transfers between devices: 1.63 us -> 2.47 us  [swap(): return lax.ppermute(x, 'gz', [(i, i ^ bits) for i in range(count)])]
    unnamed x5 -> x7, local copies, waits for them, and re-layouts: 0.79 us -> 0.8 us
  transfers between devices with their start and end apart: 7 -> 7, of which waited for: 3 -> 3; matrix products, arithmetic and copies ran while one was open for 8% -> 5% of each run, Pallas kernels for 3% -> 3%
where the time goes in v5:
time: 34.6 us; the launch traced here: 34.3 us
  Pallas kernels  22.1 us (64%)
  starting transfers between devices  6.73 us (19%)
  waiting for transfers between devices  2.47 us (7%)
  local copies, waits for them, and re-layouts  1.82 us (5%)
  other arithmetic  0.99 us (3%)
    pallas_call x1, Pallas kernels, per_device(): pl.pallas_call(functools.partial(kernel, (window, tiles)), out_shape=jax....  21.2 us
    ppermute x7, starting transfers between devices, swap(): return lax.ppermute(x, 'gz', [(i, i ^ bits) for i in range(count)])  6.73 us
    ppermute x7, waiting for transfers between devices, swap(): return lax.ppermute(x, 'gz', [(i, i ^ bits) for i in range(count)])  2.47 us
    another operation x1, local copies, waits for them, and re-layouts  0.92 us
    pallas_call x1, Pallas kernels, per_device(): pl.pallas_call(functools.partial(prepare, (dual_in.shape[::-1], primal_in...  0.92 us
    concatenate x1, other arithmetic, per_device(): jnp.concatenate([jnp.pad(p, ((0, -p.shape[0] % 16), (0, primal_hidden - p...  0.9 us
    unnamed x7, local copies, waits for them, and re-layouts  0.8 us
  transfers between devices with their start and end apart: 7, of which 3 were waited for; matrix products, arithmetic and copies ran while one was open for 5% of the time, Pallas kernels for 3%

profile of v5, /device:TPU:1, one launch (start us, length us, event | category | flops | bytes accessed | tf_op | source)
XLA Modules:
  0.0 34.3 jit_solution(5918406140023619566)
XLA Ops:
  0.0 0.0 copy-start
  0.0 0.9 %dynamic-slice_convert_fusion = (bf16[1,16,1024]{2,1,0:T(8,128)(2,1)S(1)}, bf16[1,16,1024]{2,1,0:T(8,128)(2,1)S(1)}) fusion(f32[4,16,1024]{2,1,0:T(8,128)} %param.9, s32[]{:T(128)S(6)} %select_n.2, f32[4,16,1024]{2,1,0:T(8,128)} %volumes.1), kind=kLoop, calls=%fused_computation.13 | loop fusion | bytes 131076 | tf_op jit(solution)/shard_map/convert.1
  0.9 4.2 %collective-permute-start.5 = (bf16[2,16,1024]{2,1,0:T(8,128)(2,1)S(1)}, bf16[2,16,1024]{2,1,0:T(8,128)(2,1)S(1)}, u32[]{:S(2)}, u32[]{:S(2)}) collective-permute-start(bf16[2,16,1024]{2,1,0:T(8,128)(2,1)S(1)} %pad_maximum_fusion.refs_0_), channel_id=1, source_target_pairs={{0,6},{1,7},{2,4},{3,5},{4,2},{5,3},{6,0},{7,1},{8,14},{9,15},{10,... | collective-permute-start | bytes 196616 | tf_op jit(solution)/shard_map/ppermute | solution.py:349
  5.2 0.0 collective-permute-start.3
  5.2 0.4 %collective-permute-start.1 = (bf16[2,16,1024]{2,1,0:T(8,128)(2,1)S(1)}, bf16[2,16,1024]{2,1,0:T(8,128)(2,1)S(1)}, u32[]{:S(2)}, u32[]{:S(2)}) collective-permute-start(bf16[2,16,1024]{2,1,0:T(8,128)(2,1)S(1)} %pad_maximum_fusion.refs_0_), channel_id=1, source_target_pairs={{0,2},{1,3},{2,0},{3,1},{4,6},{5,7},{6,4},{7,5},{8,10},{9,11},{10,... | collective-permute-start | bytes 196616 | tf_op jit(solution)/shard_map/ppermute | solution.py:349
  5.5 1.2 %collective-permute-start = (bf16[2,16,1024]{2,1,0:T(8,128)(2,1)S(1)}, bf16[2,16,1024]{2,1,0:T(8,128)(2,1)S(1)}, u32[]{:S(2)}, u32[]{:S(2)}) collective-permute-start(bf16[2,16,1024]{2,1,0:T(8,128)(2,1)S(1)} %pad_maximum_fusion.refs_0_), channel_id=1, source_target_pairs={{0,1},{1,0},{2,3},{3,2},{4,5},{5,4},{6,7},{7,6},{8,9},{9,8},{10,11... | collective-permute-start | bytes 196616 | tf_op jit(solution)/shard_map/ppermute | solution.py:349
  6.8 0.1 stack.40
  6.9 0.8 %copy.9 = bf16[32,27]{0,1:T(8,128)(2,1)S(1)} copy(bf16[32,27]{1,0:T(8,128)(2,1)} %param.12) | data formatting | bytes 3456 | tf_op args[4]
  7.6 0.9 %fusion.7.weights = bf16[144,64]{1,0:T(8,128)(2,1)S(1)} fusion(bf16[27,64]{1,0:T(8,128)(2,1)} %param.15, bf16[54,64]{1,0:T(8,128)(2,1)} %bitcast.17, bf16[9,32]{1,0:T(8,128)(2,1)} %param.13, bf16[27,32]{1,0:T(8,128)(2,1)S(1)} %bitcast.16), kind=kLoop, calls=%fused_computation.16 | loop fusion | flops 184320 | bytes 31104 | tf_op jit(solution)/shard_map/concatenate | solution.py:381
  8.5 0.9 %prepare.1 = (bf16[256,96]{1,0:T(8,128)(2,1)S(1)}, bf16[48,256]{1,0:T(8,128)(2,1)S(1)}, bf16[512,224]{1,0:T(8,128)(2,1)S(1)}, bf16[144,512]{1,0:T(8,128)(2,1)S(1)}) custom-call(bf16[144,64]{1,0:T(8,128)(2,1)S(1)} %fusion.7.weights), custom_call_target="tpu_custom_call" | custom-call | flops 2000000000 | bytes 8000000 | tf_op jit(solution)/shard_map/prepare/pallas_call | solution.py:388
  9.5 0.0 copy-done
  9.5 0.0 collective-permute-done.5.refs_6_
  9.5 0.1 collective-permute-start.6
  9.6 1.3 %collective-permute-done.3.refs_4_ = bf16[2,16,1024]{2,1,0:T(8,128)(2,1)S(1)} collective-permute-done((bf16[2,16,1024]{2,1,0:T(8,128)(2,1)S(1)}, bf16[2,16,1024]{2,1,0:T(8,128)(2,1)S(1)}, u32[]{:S(2)}, u32[]{:S(2)}) %collective-permute-start.3) | collective-permute-done | bytes 65568 | tf_op jit(solution)/shard_map/ppermute | solution.py:349
  10.9 0.8 %collective-permute-start.4 = (bf16[2,16,1024]{2,1,0:T(8,128)(2,1)S(1)}, bf16[2,16,1024]{2,1,0:T(8,128)(2,1)S(1)}, u32[]{:S(2)}, u32[]{:S(2)}) collective-permute-start(bf16[2,16,1024]{2,1,0:T(8,128)(2,1)S(1)} %collective-permute-done.3.refs_4_), channel_id=1, source_target_pairs={{0,1},{1,0},{2,3},{3,2},{4,5},{5,4},{6,7},{7,6},{8,9},{9,8},{10,11... | collective-permute-start | bytes 196616 | tf_op jit(solution)/shard_map/ppermute | solution.py:349
  11.7 0.0 collective-permute-done.1.refs_2_
  11.7 0.0 collective-permute-start.2
  11.7 0.1 pad_add_fusion.info
  11.8 0.0 collective-permute-done.refs_1_
  11.8 0.0 collective-permute-done.6.refs_7_
  11.8 0.8 %collective-permute-done.4.refs_5_ = bf16[2,16,1024]{2,1,0:T(8,128)(2,1)S(1)} collective-permute-done((bf16[2,16,1024]{2,1,0:T(8,128)(2,1)S(1)}, bf16[2,16,1024]{2,1,0:T(8,128)(2,1)S(1)}, u32[]{:S(2)}, u32[]{:S(2)}) %collective-permute-start.4) | collective-permute-done | bytes 65568 | tf_op jit(solution)/shard_map/ppermute | solution.py:349
  12.6 0.4 %collective-permute-done.2.refs_3_ = bf16[2,16,1024]{2,1,0:T(8,128)(2,1)S(1)} collective-permute-done((bf16[2,16,1024]{2,1,0:T(8,128)(2,1)S(1)}, bf16[2,16,1024]{2,1,0:T(8,128)(2,1)S(1)}, u32[]{:S(2)}, u32[]{:S(2)}) %collective-permute-start.2) | collective-permute-done | bytes 65568 | tf_op jit(solution)/shard_map/ppermute | solution.py:349
  13.0 0.0 copy-done.2
  13.0 21.2 %iterate.1 = f32[16,1024]{1,0:T(8,128)} custom-call(s32[18]{0:T(128)S(1)} %pad_add_fusion.info, f32[4,16,1024]{2,1,0:T(8,128)S(1)} %copy-done.2, bf16[2,16,1024]{2,1,0:T(8,128)(2,1)S(1)} %pad_maximum_fusion.refs_0_, bf16[2,16,1024]{2,1,0:T(8,128)(2,1)S(1)} %collective-permute-done.refs_1_, bf16[2,16,1024]{2,1,0:T(8,128)(2,1)S(1)} %collective-permute-done.1.refs_2_, ...), custom_call_target="tpu_custom_call" | custom-call | tf_op jit(solution)/shard_map/iterate/pallas_call | solution.py:402
  (6 shorter events, 0.0 us)
Async XLA Ops:
  0.0 9.5 %copy-start = (s32[4,8]{1,0:T(4,128)S(1)}, s32[4,8]{1,0:T(4,128)}, u32[]{:S(2)}) copy-start(s32[4,8]{1,0:T(4,128)} %param.10) | copy-start | bytes 388
  0.0 13.0 %copy-start.2 = (f32[4,16,1024]{2,1,0:T(8,128)S(1)}, f32[4,16,1024]{2,1,0:T(8,128)}, u32[]{:S(2)}) copy-start(f32[4,16,1024]{2,1,0:T(8,128)} %volumes.1) | copy-start | bytes 786436
  0.9 8.6 %collective-permute-start.5 = (bf16[2,16,1024]{2,1,0:T(8,128)(2,1)S(1)}, bf16[2,16,1024]{2,1,0:T(8,128)(2,1)S(1)}, u32[]{:S(2)}, u32[]{:S(2)}) collective-permute-start(bf16[2,16,1024]{2,1,0:T(8,128)(2,1)S(1)} %pad_maximum_fusion.refs_0_), channel_id=1, source_target_pairs={{0,6},{1,7},{2,4},{3,5},{4,2},{5,3},{6,0},{7,1},{8,14},{9,15},{10,... | collective-permute-start | bytes 196616 | tf_op jit(solution)/shard_map/ppermute | solution.py:349
  5.2 5.7 %collective-permute-start.3 = (bf16[2,16,1024]{2,1,0:T(8,128)(2,1)S(1)}, bf16[2,16,1024]{2,1,0:T(8,128)(2,1)S(1)}, u32[]{:S(2)}, u32[]{:S(2)}) collective-permute-start(bf16[2,16,1024]{2,1,0:T(8,128)(2,1)S(1)} %pad_maximum_fusion.refs_0_), channel_id=1, source_target_pairs={{0,4},{1,5},{2,6},{3,7},{4,0},{5,1},{6,2},{7,3},{8,12},{9,13},{10,... | collective-permute-start | bytes 196616 | tf_op jit(solution)/shard_map/ppermute | solution.py:349
  5.2 6.6 %collective-permute-start.1 = (bf16[2,16,1024]{2,1,0:T(8,128)(2,1)S(1)}, bf16[2,16,1024]{2,1,0:T(8,128)(2,1)S(1)}, u32[]{:S(2)}, u32[]{:S(2)}) collective-permute-start(bf16[2,16,1024]{2,1,0:T(8,128)(2,1)S(1)} %pad_maximum_fusion.refs_0_), channel_id=1, source_target_pairs={{0,2},{1,3},{2,0},{3,1},{4,6},{5,7},{6,4},{7,5},{8,10},{9,11},{10,... | collective-permute-start | bytes 196616 | tf_op jit(solution)/shard_map/ppermute | solution.py:349
  5.5 6.3 %collective-permute-start = (bf16[2,16,1024]{2,1,0:T(8,128)(2,1)S(1)}, bf16[2,16,1024]{2,1,0:T(8,128)(2,1)S(1)}, u32[]{:S(2)}, u32[]{:S(2)}) collective-permute-start(bf16[2,16,1024]{2,1,0:T(8,128)(2,1)S(1)} %pad_maximum_fusion.refs_0_), channel_id=1, source_target_pairs={{0,1},{1,0},{2,3},{3,2},{4,5},{5,4},{6,7},{7,6},{8,9},{9,8},{10,11... | collective-permute-start | bytes 196616 | tf_op jit(solution)/shard_map/ppermute | solution.py:349
  7.6 5.3 %copy-start.1 = (bf16[3,1024,1024]{2,1,0:T(8,128)(2,1)S(1)}, bf16[3,1024,1024]{2,1,0:T(8,128)(2,1)}, u32[]{:S(2)}) copy-start(bf16[3,1024,1024]{2,1,0:T(8,128)(2,1)} %param.11) | copy-start | bytes 18874372
  9.5 2.3 %collective-permute-start.6 = (bf16[2,16,1024]{2,1,0:T(8,128)(2,1)S(1)}, bf16[2,16,1024]{2,1,0:T(8,128)(2,1)S(1)}, u32[]{:S(2)}, u32[]{:S(2)}) collective-permute-start(bf16[2,16,1024]{2,1,0:T(8,128)(2,1)S(1)} %collective-permute-done.5.refs_6_), channel_id=1, source_target_pairs={{0,1},{1,0},{2,3},{3,2},{4,5},{5,4},{6,7},{7,6},{8,9},{9,8},{10,11... | collective-permute-start | bytes 196616 | tf_op jit(solution)/shard_map/ppermute | solution.py:349
  10.9 1.7 %collective-permute-start.4 = (bf16[2,16,1024]{2,1,0:T(8,128)(2,1)S(1)}, bf16[2,16,1024]{2,1,0:T(8,128)(2,1)S(1)}, u32[]{:S(2)}, u32[]{:S(2)}) collective-permute-start(bf16[2,16,1024]{2,1,0:T(8,128)(2,1)S(1)} %collective-permute-done.3.refs_4_), channel_id=1, source_target_pairs={{0,1},{1,0},{2,3},{3,2},{4,5},{5,4},{6,7},{7,6},{8,9},{9,8},{10,11... | collective-permute-start | bytes 196616 | tf_op jit(solution)/shard_map/ppermute | solution.py:349
  11.7 1.3 %collective-permute-start.2 = (bf16[2,16,1024]{2,1,0:T(8,128)(2,1)S(1)}, bf16[2,16,1024]{2,1,0:T(8,128)(2,1)S(1)}, u32[]{:S(2)}, u32[]{:S(2)}) collective-permute-start(bf16[2,16,1024]{2,1,0:T(8,128)(2,1)S(1)} %collective-permute-done.1.refs_2_), channel_id=1, source_target_pairs={{0,1},{1,0},{2,3},{3,2},{4,5},{5,4},{6,7},{7,6},{8,9},{9,8},{10,11... | collective-permute-start | bytes 196616 | tf_op jit(solution)/shard_map/ppermute | solution.py:349
